TPU v7x, 32 devices: a whole 2x2x4 slice. The times are simulated.
32 devices in a mesh: seq: 8 (over y, x, core), tensor: 4 (over z).
Axes of the slice: x: 2, y: 2, z: 4, core: 2. Of those that a mesh axis runs over, the one named last changes fastest.
Arguments:
- weight: bfloat16 [16384, 5376], P(('seq', 'tensor')), may hold values from -2.2 to 2.2
- hidden: bfloat16 [64, 5376], P('seq'), may hold values from -3.2 to 3.2
- targets: int32 [64], replicated, may hold values from 0 to 16383
- branch: int32 [64], replicated, may hold values from 0 to 2
- pair_of_row: int32 [64], replicated, may hold values from 0 to 15, never falling along the last dimension, each value on 1 to 12 neighbouring positions
- ref_log_prob: float32 [64], replicated, may hold values from -20 to -12
- pair_weight: float32 [16], replicated, may hold values from 2 to 16
- token_ids: int32 [6400], P(('seq', 'tensor')), may hold values from 0 to 16383, as said below
- token_grad: bfloat16 [6400, 5376], P(('seq', 'tensor')), may hold values from -0.059814453 to 0.059814453
Outputs:
- dpo_loss: float32 [], replicated
- weight_grad: bfloat16 [16384, 5376], P(('seq', 'tensor'))
- hidden_grad: bfloat16 [64, 5376], P('seq')
Inputs may be any that keep to these rules, and one draw needn't show every extreme that they name: `token_ids`: ids of one device's 200 rows fall at most 13 times into the 512 vocabulary rows of any one device; in every draw one such block of vocabulary rows receives exactly 13 ids from every device.
All inputs are finite; a program needn't handle non-finite values.
Results may differ from a plain program's by a relative error of at most 0.007.
Values may be sent and summed in bfloat16 or wider, within the bound.
A program may use at most 128 MiB of HBM per device.

v0:
```python
import math

import jax
import jax.numpy as jnp
from jax import lax
from jax.sharding import PartitionSpec as P

dpo_beta = 0.1


def shards(
    weight, hidden, targets, branch, pair_of_row, ref_log_prob, pair_weight, token_ids, token_grad
):
    vocab_rows, model_width = weight.shape
    seq_count = lax.axis_size("seq")
    tensor_count = lax.axis_size("tensor")
    owners = seq_count * tensor_count
    vocab_start = lax.axis_index(("seq", "tensor")) * vocab_rows
    gathered = lax.all_gather(hidden, "seq", axis=0, tiled=True)
    logits = lax.dot_general(
        gathered, weight, (((1,), (1,)), ((), ())), preferred_element_type=jnp.float32
    )
    columns = jnp.arange(vocab_rows, dtype=jnp.int32)
    target_hit = (columns[None, :] == (targets - vocab_start)[:, None]).astype(jnp.float32)
    target_part = jnp.sum(logits * target_hit, axis=1)
    row_top = lax.pmax(jnp.max(logits, axis=1), ("seq", "tensor"))
    shifted = jnp.exp(logits - row_top[:, None])
    row_total, target_logit = lax.psum((jnp.sum(shifted, axis=1), target_part), ("seq", "tensor"))
    log_prob = target_logit - row_top - jnp.log(row_total)
    branch_sign = (branch == 1).astype(jnp.float32) - (branch == 2).astype(jnp.float32)
    pair_count = pair_weight.shape[0]
    member = (pair_of_row[:, None] == jnp.arange(pair_count, dtype=jnp.int32)[None, :]).astype(
        jnp.float32
    )
    margin = jnp.sum(member * (branch_sign * (log_prob - ref_log_prob))[:, None], axis=0)
    dpo_loss = jnp.sum(pair_weight * jax.nn.softplus(-dpo_beta * margin))
    push_back = pair_weight * jax.nn.sigmoid(-dpo_beta * margin)
    row_scale = -dpo_beta * branch_sign * jnp.sum(member * push_back[None, :], axis=1)
    probs = shifted / row_total[:, None]
    dlogits = (row_scale[:, None] * (target_hit - probs)).astype(jnp.bfloat16)
    head_grad = lax.dot_general(
        dlogits, gathered, (((0,), (0,)), ((), ())), preferred_element_type=jnp.float32
    )
    partial_value = lax.psum_scatter(
        jnp.dot(dlogits, weight, preferred_element_type=jnp.float32),
        "seq",
        scatter_dimension=0,
        tiled=True,
    )
    hidden_grad = lax.psum(partial_value, "tensor").astype(jnp.bfloat16)
    token_count = token_ids.shape[0]
    capacity = max(2, (2 * token_count + owners - 1) // owners)
    row_owner = token_ids // vocab_rows
    position = jnp.arange(token_count, dtype=jnp.int32)
    earlier = (row_owner[:, None] == row_owner[None, :]) & (position[None, :] < position[:, None])
    bucket_slot = jnp.sum(earlier.astype(jnp.int32), axis=1)
    landing = row_owner * capacity + bucket_slot
    outgoing = jnp.zeros((owners * capacity, model_width), jnp.bfloat16).at[landing].set(token_grad)
    labels = (
        jnp.full((owners * capacity,), -1, jnp.int32)
        .at[landing]
        .set(token_ids - row_owner * vocab_rows)
    )
    outgoing = outgoing.reshape(seq_count, tensor_count, capacity, model_width)
    labels = labels.reshape(seq_count, tensor_count, capacity)
    arrived = lax.all_to_all(
        lax.all_to_all(outgoing, "seq", split_axis=0, concat_axis=0, tiled=True),
        "tensor",
        split_axis=1,
        concat_axis=1,
        tiled=True,
    )
    arrived_ids = lax.all_to_all(
        lax.all_to_all(labels, "seq", split_axis=0, concat_axis=0, tiled=True),
        "tensor",
        split_axis=1,
        concat_axis=1,
        tiled=True,
    )
    arrived = arrived.reshape(owners * capacity, model_width)
    arrived_ids = arrived_ids.reshape(owners * capacity)
    onehot = (columns[:, None] == arrived_ids[None, :]).astype(jnp.bfloat16)
    embed_grad = jnp.dot(onehot, arrived, preferred_element_type=jnp.float32)
    weight_grad = (head_grad + math.sqrt(model_width) * embed_grad).astype(jnp.bfloat16)
    return (dpo_loss, weight_grad, hidden_grad)


def solution(mesh):
    return jax.shard_map(
        shards,
        mesh=mesh,
        in_specs=(
            P(("seq", "tensor"), None),
            P("seq", None),
            P(),
            P(),
            P(),
            P(),
            P(),
            P(("seq", "tensor")),
            P(("seq", "tensor"), None),
        ),
        out_specs=(P(), P(("seq", "tensor"), None), P("seq", None)),
        check_vma=False,
    )
```

profile of v0, /device:TPU:0, one launch (start us, length us, event | category | flops | bytes accessed | tf_op | source)
XLA Modules:
  0.0 357.9 jit_solution(12325973842113832220)
XLA Ops:
  7.2 0.7 multiply_subtract_fusion
  8.1 1.2 scatter_custom_fusion
  9.3 0.7 reshape.25
  10.0 5.2 %all-to-all-start = ((s32[8,4,13]{2,1,0:T(4,128)}), s32[8,4,13]{2,1,0:T(4,128)S(1)}, u32[]{:S(2)}, u32[]{:S(2)}) async-start(s32[8,4,13]{2,1,0:T(4,128)} %reshape.25), calls=%async_computation | async-start | bytes 32768 | tf_op jit(solution)/shard_map/all_to_all | solution.py:74
  15.2 7.3 %scatter_custom_fusion.1 = bf16[416,5376]{1,0:T(8,128)(2,1)} fusion(s32[200]{0:T(256)S(1)} %compare_select_fusion, bf16[200,5376]{1,0:T(8,128)(2,1)} %param.17, bf16[]{:T(256)} %constant.55.clone.1), kind=kCustom, calls=%fused_computation.3 | custom fusion | bytes 4473344 | tf_op jit(solution)/shard_map/scatter | solution.py:58
  22.4 5.8 %reshape.26 = bf16[8,4,13,5376]{3,2,1,0:T(8,128)(2,1)} reshape(bf16[416,5376]{1,0:T(8,128)(2,1)} %scatter_custom_fusion.1) | data formatting | bytes 8945664 | tf_op jit(solution)/shard_map/reshape | solution.py:64
  28.2 7.1 %copy.22 = bf16[8,4,13,5376]{3,1,2,0:T(4,128)(2,1)} copy(bf16[8,4,13,5376]{3,2,1,0:T(8,128)(2,1)} %reshape.26) | data formatting | bytes 8945664 | tf_op jit(solution)/shard_map/reshape | solution.py:64
  35.3 4.6 %all-to-all-start.2 = ((bf16[8,4,13,5376]{3,1,2,0:T(4,128)(2,1)}), bf16[8,4,13,5376]{3,1,2,0:T(4,128)(2,1)}, u32[]{:S(2)}, u32[]{:S(2)}) async-start(bf16[8,4,13,5376]{3,1,2,0:T(4,128)(2,1)} %copy.22), calls=%async_computation.2 | async-start | bytes 8945664 | tf_op jit(solution)/shard_map/all_to_all | solution.py:67
  40.5 51.5 %all-to-all-done.2 = bf16[8,4,13,5376]{3,1,2,0:T(4,128)(2,1)} async-done(((bf16[8,4,13,5376]{3,1,2,0:T(4,128)(2,1)}), bf16[8,4,13,5376]{3,1,2,0:T(4,128)(2,1)}, u32[]{:S(2)}, u32[]{:S(2)}) %all-to-all-start.2) | async-done | bytes 4472864 | tf_op jit(solution)/shard_map/all_to_all | solution.py:67
  92.0 4.9 %all-to-all-start.1 = ((s32[8,4,13]{2,0,1:T(8,128)}), s32[8,4,13]{2,0,1:T(8,128)S(1)}, u32[]{:S(2)}, u32[]{:S(2)}) async-start(s32[8,4,13]{2,0,1:T(8,128)} %copy.20), calls=%async_computation.1 | async-start | bytes 32768 | tf_op jit(solution)/shard_map/all_to_all | solution.py:73
  96.9 4.8 %copy.23 = bf16[8,4,13,5376]{3,0,2,1:T(8,128)(2,1)} copy(bf16[8,4,13,5376]{3,1,2,0:T(4,128)(2,1)} %all-to-all-done.2) | data formatting | bytes 8945664 | tf_op jit(solution)/shard_map/all_to_all | solution.py:67
  101.7 0.8 all-to-all-done.1
  102.5 4.9 %all-to-all-start.3 = ((bf16[8,4,13,5376]{3,0,2,1:T(8,128)(2,1)}), bf16[8,4,13,5376]{3,0,2,1:T(8,128)(2,1)}, u32[]{:S(2)}, u32[]{:S(2)}) async-start(bf16[8,4,13,5376]{3,0,2,1:T(8,128)(2,1)} %copy.23), calls=%async_computation.3 | async-start | bytes 8945664 | tf_op jit(solution)/shard_map/all_to_all | solution.py:66
  107.5 9.3 %all_gather.3 = bf16[64,5376]{1,0:T(8,128)(2,1)S(1)} all-gather(bf16[8,5376]{1,0:T(8,128)(2,1)S(1)} %copy-done), channel_id=1, replica_groups=mesh['seq'=8,'tensor'=4] {'seq'}, dimensions={0}, use_global_device_ids=true | all-gather | bytes 774144 | tf_op jit(solution)/shard_map/all_gather | solution.py:19
  116.8 4.4 %fusion.12 = (f32[64]{0:T(128)S(1)}, f32[64,512]{1,0:T(8,128)S(1)}) fusion(bf16[64,5376]{1,0:T(8,128)(2,1)S(1)} %all_gather.3, bf16[512,5376]{1,0:T(8,128)(2,1)} %param.9), kind=kOutput, calls=%fused_computation.38 | convolution fusion | flops 352354240 | bytes 6324480 | tf_op jit(solution)/shard_map/dot_general | solution.py:20
  121.3 103.0 %pmax.7 = f32[64]{0:T(128)S(1)} all-reduce(f32[64]{0:T(128)S(1)} %get-tuple-element.11), channel_id=1, replica_groups=mesh['seq'=8,'tensor'=4] {'seq','tensor'}, use_global_device_ids=true, to_apply=%region_3.0 | all-reduce | flops 64 | bytes 512 | tf_op jit(solution)/shard_map/pmax | solution.py:26
  224.5 39.6 %all-reduce = (f32[64]{0:T(128)S(1)}, f32[64]{0:T(128)S(1)}) all-reduce(f32[64]{0:T(128)S(1)} %get-tuple-element.4, f32[64]{0:T(128)S(1)} %get-tuple-element.3), channel_id=1, replica_groups=mesh['seq'=8,'tensor'=4] {'seq','tensor'}, use_global_device_ids=true, to_apply=%region_5.0 | all-reduce | flops 128 | bytes 1024 | tf_op jit(solution)/shard_map/psum | solution.py:28
  264.9 4.8 %fusion.10 = f32[64,5376]{1,0:T(8,128)} fusion(bf16[512,5376]{1,0:T(8,128)(2,1)} %param.9, f32[64,512]{1,0:T(8,128)S(1)} %get-tuple-element.12, f32[64]{0:T(128)S(1)} %get-tuple-element.5, f32[64]{0:T(128)S(1)} %multiply_multiply_fusion, f32[64]{0:T(128)S(1)} %pmax.7, s32[64]{0:T(128)S(1)} %broadcast_subtract_fusion), kind=kOutput, calls=%fused_computation.36 | convolution fusion | flops 352550912 | bytes 7013376 | tf_op jit(solution)/shard_map/dot_general | solution.py:45
  269.7 5.9 %fusion.11 = f32[512,5376]{1,0:T(8,128)} fusion(bf16[64,5376]{1,0:T(8,128)(2,1)S(1)} %all_gather.3, f32[64,512]{1,0:T(8,128)S(1)} %get-tuple-element.12, f32[64]{0:T(128)S(1)} %get-tuple-element.5, f32[64]{0:T(128)S(1)} %multiply_multiply_fusion, f32[64]{0:T(128)S(1)} %pmax.7, s32[64]{0:T(128)S(1)} %broadcast_subtract_fusion), kind=kOutput, calls=%fused_computation.37 | convolution fusion | flops 352550912 | bytes 11830272 | tf_op jit(solution)/shard_map/dot_general | solution.py:41
  275.7 32.2 %reduce-scatter.2.cloned.1.call-done = f32[8,5376]{1,0:T(8,128)} async-done(((f32[64,5376]{1,0:T(8,128)}), f32[8,5376]{1,0:T(8,128)}) %reduce-scatter.2.cloned.1.call-update) | async-done | bytes 172048 | tf_op jit(solution)/shard_map/reduce_scatter | solution.py:44
  307.9 23.1 %all-reduce.2 = bf16[8,5376]{1,0:T(8,128)(2,1)} all-reduce(f32[8,5376]{1,0:T(8,128)} %reduce-scatter.2.cloned.1.call-done), channel_id=1, replica_groups=mesh['seq'=8,'tensor'=4] {'tensor'}, use_global_device_ids=true, to_apply=%region_13.14 | all-reduce | flops 43008 | bytes 258048 | tf_op jit(solution)/shard_map/psum | solution.py:50
  331.0 5.6 %copy.24 = bf16[8,4,13,5376]{3,2,1,0:T(8,128)(2,1)} copy(bf16[8,4,13,5376]{3,0,2,1:T(8,128)(2,1)} %all-to-all-done.3) | data formatting | bytes 8945664 | tf_op jit(solution)/shard_map/all_to_all | solution.py:66
  336.6 5.8 %reshape.27 = bf16[416,5376]{1,0:T(8,128)(2,1)} reshape(bf16[8,4,13,5376]{3,2,1,0:T(8,128)(2,1)} %copy.24) | data formatting | bytes 8945664 | tf_op jit(solution)/shard_map/reshape | solution.py:80
  342.4 8.7 %add_convert_fusion = bf16[512,5376]{1,0:T(8,128)(2,1)} fusion(f32[512,5376]{1,0:T(8,128)} %fusion.11, bf16[416,5376]{1,0:T(8,128)(2,1)} %reshape.27, s32[416]{0:T(512)S(1)} %eq.80), kind=kOutput, calls=%fused_computation.2 | convolution fusion | flops 2298560512 | bytes 20989568 | tf_op jit(solution)/shard_map/dot_general | solution.py:83
  (28 shorter events, 2.1 us)
Async XLA Ops:
  10.0 25.3 %all-to-all-start = ((s32[8,4,13]{2,1,0:T(4,128)}), s32[8,4,13]{2,1,0:T(4,128)S(1)}, u32[]{:S(2)}, u32[]{:S(2)}) async-start(s32[8,4,13]{2,1,0:T(4,128)} %reshape.25), calls=%async_computation | async-start | bytes 32768 | tf_op jit(solution)/shard_map/all_to_all | solution.py:74
  35.3 56.7 %all-to-all-start.2 = ((bf16[8,4,13,5376]{3,1,2,0:T(4,128)(2,1)}), bf16[8,4,13,5376]{3,1,2,0:T(4,128)(2,1)}, u32[]{:S(2)}, u32[]{:S(2)}) async-start(bf16[8,4,13,5376]{3,1,2,0:T(4,128)(2,1)} %copy.22), calls=%async_computation.2 | async-start | bytes 8945664 | tf_op jit(solution)/shard_map/all_to_all | solution.py:67
  92.0 10.5 %all-to-all-start.1 = ((s32[8,4,13]{2,0,1:T(8,128)}), s32[8,4,13]{2,0,1:T(8,128)S(1)}, u32[]{:S(2)}, u32[]{:S(2)}) async-start(s32[8,4,13]{2,0,1:T(8,128)} %copy.20), calls=%async_computation.1 | async-start | bytes 32768 | tf_op jit(solution)/shard_map/all_to_all | solution.py:73
  101.7 5.8 %copy-start = (bf16[8,5376]{1,0:T(8,128)(2,1)S(1)}, bf16[8,5376]{1,0:T(8,128)(2,1)}, u32[]{:S(2)}) copy-start(bf16[8,5376]{1,0:T(8,128)(2,1)} %param.10) | copy-start | bytes 258052
  102.5 228.5 %all-to-all-start.3 = ((bf16[8,4,13,5376]{3,0,2,1:T(8,128)(2,1)}), bf16[8,4,13,5376]{3,0,2,1:T(8,128)(2,1)}, u32[]{:S(2)}, u32[]{:S(2)}) async-start(bf16[8,4,13,5376]{3,0,2,1:T(8,128)(2,1)} %copy.23), calls=%async_computation.3 | async-start | bytes 8945664 | tf_op jit(solution)/shard_map/all_to_all | solution.py:66
  107.4 116.9 %copy-start.4 = (s32[64]{0:T(128)S(1)}, s32[64]{0:T(128)}, u32[]{:S(2)}) copy-start(s32[64]{0:T(128)} %param.11) | copy-start | bytes 772
  107.4 156.6 %copy-start.1 = (f32[64]{0:T(128)S(1)}, f32[64]{0:T(128)}, u32[]{:S(2)}) copy-start(f32[64]{0:T(128)} %param.14) | copy-start | bytes 772
  107.4 156.6 %copy-start.3 = (s32[64]{0:T(128)S(1)}, s32[64]{0:T(128)}, u32[]{:S(2)}) copy-start(s32[64]{0:T(128)} %param.12) | copy-start | bytes 772
  107.4 156.6 %copy-start.5 = (s32[64]{0:T(128)S(1)}, s32[64]{0:T(128)}, u32[]{:S(2)}) copy-start(s32[64]{0:T(128)} %param.13) | copy-start | bytes 772
  107.4 156.7 %copy-start.2 = (f32[16]{0:T(128)S(1)}, f32[16]{0:T(128)}, u32[]{:S(2)}) copy-start(f32[16]{0:T(128)} %param.15) | copy-start | bytes 196
  107.4 200.4 %reduce-scatter.2.cloned.1.call-start = ((), (), s32[]{:S(2)}) async-start(), calls=%async_computation.5 | async-start | bytes 1548288 | tf_op jit(solution)/shard_map/reduce_scatter | solution.py:44
Sparse Core Ops, SparseCore 0:
  269.8 38.0 reduce-scatter.1
where the time goes:
time: 359 us; the launch traced here: 358 us
  blocking collectives  175 us (49%)
  waiting for transfers between devices  84.5 us (24%)
  local copies, waits for them, and re-layouts  39 us (11%)
  matrix products  23.7 us (7%)
  starting transfers between devices  19.5 us (5%)
  between operations  14.1 us (4%)
    pmax x1, blocking collectives, shards(): row_top = lax.pmax(jnp.max(logits, axis=1), ('seq', 'tensor'))  103 us
    all_to_all x1, waiting for transfers between devices, shards(): lax.all_to_all(outgoing, 'seq', split_axis=0, concat_axis=0, tiled=True)  51.5 us
    psum x1, blocking collectives, shards(): lax.psum((jnp.sum(shifted, axis=1), target_part), ('seq', 'tensor'))  39.6 us
    reduce_scatter x1, waiting for transfers between devices, shards(): lax.psum_scatter(jnp.dot(dlogits, weight, preferred_element_type=jnp.floa...  32.2 us
    psum x1, blocking collectives, shards(): hidden_grad = lax.psum(partial_value, 'tensor').astype(jnp.bfloat16)  23.1 us
    reshape x2, local copies, waits for them, and re-layouts, shards(): outgoing = outgoing.reshape(seq_count, tensor_count, capacity, model_width)  12.9 us
    all_gather x1, blocking collectives, shards(): gathered = lax.all_gather(hidden, 'seq', axis=0, tiled=True)  9.3 us
    dot_general x1, matrix products, shards(): embed_grad = jnp.dot(onehot, arrived, preferred_element_type=jnp.float32)  8.65 us
  transfers between devices with their start and end apart: 5, of which 3 were waited for; matrix products, arithmetic and copies ran while one was open for 12% of the time, Pallas kernels for 0%

commit v1 on v0

v1 whole, which is shorter than its diff:
```python
import functools
import math

import jax
import jax.numpy as jnp
from jax import lax
from jax.experimental import pallas as pl
from jax.experimental.pallas import tpu as pltpu
from jax.sharding import PartitionSpec as P

dpo_beta = 0.1
LANES = 128
ROWS = 16
CHUNK = 128
MESH = pl.DeviceIdType.MESH
F32, BF16 = jnp.float32, jnp.bfloat16


def pack_plan(capacity, tiles):
    for piece in range(tiles // 2, 0, -1):
        parts = tiles // piece - 1
        if tiles % piece == 0 and (ROWS - capacity) * parts >= capacity:
            return piece, parts
    raise ValueError("no packing")


def exchange_kernel(
    seq, tensor, capacity, piece, parts,
    targets, branch, pair_of_row, ref_log_prob, pair_weight, ids_row, ids_col, hidden, token_grad, weight_hbm,
    arrived, arrived_labels, dlogits, gathered, hidden_grad, loss,
    weight, packed, labels, folded, logits, stat, stats, partial, seq_parts, sums, tensor_parts, done, pieces,
    load_sem, own_sem, send_sems, recv_sems,
):
    n = seq * tensor
    vocab_rows, width = weight.shape
    resp = targets.shape[1]
    tokens = ids_row.shape[1]
    mine_seq, mine_tensor = lax.axis_index("seq"), lax.axis_index("tensor")
    me = mine_seq * tensor + mine_tensor

    def device(rel):
        peer = lax.rem(me + rel, n)
        return (lax.div(peer, tensor), lax.rem(peer, tensor))

    def send(src, dst, kind, target):
        pltpu.make_async_remote_copy(
            src_ref=src, dst_ref=dst, send_sem=send_sems.at[kind], recv_sem=recv_sems.at[kind],
            device_id=target, device_id_type=MESH,
        ).start()

    def wait(sems, kind, ref):
        pltpu.make_async_copy(ref, ref, sems.at[kind]).wait()

    load = pltpu.make_async_copy(weight_hbm, weight, load_sem)
    load.start()
    barrier = pltpu.get_barrier_semaphore()

    def greet(rel, carry):
        pl.semaphore_signal(barrier, inc=1, device_id=device(rel), device_id_type=MESH)
        return carry

    lax.fori_loop(1, n, greet, 0)

    shift = vocab_rows.bit_length() - 1
    owner = jnp.right_shift(ids_row[...], shift)
    owner_col = jnp.right_shift(ids_col[...], shift)
    before = lax.broadcasted_iota(jnp.int32, (tokens, tokens), 0) < lax.broadcasted_iota(
        jnp.int32, (tokens, tokens), 1
    )
    slot = jnp.sum(jnp.where((owner_col == owner) & before, 1.0, 0.0), axis=0, keepdims=True).astype(jnp.int32)
    rel_owner = owner - me
    rel_owner = jnp.where(rel_owner < 0, rel_owner + n, rel_owner)
    spare = jnp.zeros_like(slot)
    for j in range(1, ROWS - capacity):
        spare = spare + jnp.where(slot >= j * parts, 1, 0)
    part_of = slot - spare * parts
    main_row = rel_owner * ROWS + slot
    spare_row = rel_owner * ROWS + capacity + spare
    label = (ids_row[...] - owner * vocab_rows + 1).astype(F32)
    piece_width = piece * LANES

    pl.semaphore_wait(barrier, n - 1)

    mine_rows = pl.ds(pl.multiple_of(mine_seq * ROWS, ROWS), ROWS)
    folded[mine_rows] = hidden[...]
    for k in range(1, seq):
        send(hidden, folded.at[mine_rows], 0, (lax.rem(mine_seq + k, seq), mine_tensor))

    def pack(chunk, carry):
        base = pl.multiple_of(chunk * CHUNK, CHUNK)
        rows = base + lax.broadcasted_iota(jnp.int32, (CHUNK, tokens), 0)
        lane = lax.broadcasted_iota(jnp.int32, (CHUNK, LANES), 1)
        main = rows == main_row
        in_spare = rows == spare_row
        main_pick = jnp.where(main, 1.0, 0.0).astype(BF16)
        tags = jnp.where(lane == 0, jnp.sum(jnp.where(main, label, 0.0), axis=1, keepdims=True), 0.0)
        for part in range(parts):
            last = in_spare & (part_of == part)
            last_pick = jnp.where(last, 1.0, 0.0).astype(BF16)
            tags = jnp.where(
                lane == part + 1, jnp.sum(jnp.where(last, label, 0.0), axis=1, keepdims=True), tags
            )
            here = pl.ds(part * piece_width, piece_width)
            packed[pl.ds(base, CHUNK), here] = (
                jnp.dot(main_pick, token_grad[:, here], preferred_element_type=F32)
                + jnp.dot(
                    last_pick, token_grad[:, parts * piece_width :], preferred_element_type=F32
                )
            ).astype(BF16)
        labels[pl.ds(base, CHUNK), :] = tags

        def send_block(i, inner):
            rel = chunk * (CHUNK // ROWS) + i
            block = pl.ds(pl.multiple_of(rel * ROWS, ROWS), ROWS)

            @pl.when(rel > 0)
            def _():
                send(packed.at[block], arrived.at[block], 1, device(rel))
                send(labels.at[block], arrived_labels.at[block], 2, device(rel))

            return inner

        lax.fori_loop(0, CHUNK // ROWS, send_block, 0)
        return carry

    lax.fori_loop(0, n * ROWS // CHUNK, pack, 0)
    own = pltpu.make_async_copy(packed.at[pl.ds(0, ROWS)], arrived.at[pl.ds(0, ROWS)], own_sem)
    own.start()
    arrived_labels[pl.ds(0, ROWS), :] = labels[pl.ds(0, ROWS), :]

    wait(recv_sems, 0, folded.at[pl.ds(0, (seq - 1) * ROWS)])
    half = width // 2
    for pair in range(seq // 2):
        both = folded[pair * 2 * ROWS : (pair + 1) * 2 * ROWS].astype(F32)
        rows = pl.ds(pair * ROWS, ROWS)
        gathered[rows, :half] = jnp.concatenate([both[0:8], both[16:24]], axis=0).astype(BF16)
        gathered[rows, half:] = jnp.concatenate([both[8:16], both[24:32]], axis=0).astype(BF16)
    load.wait()
    step = 6 * LANES
    logits[...] = jnp.zeros_like(logits)

    def add_logits(i, carry):
        columns = pl.ds(pl.multiple_of(i * step, step), step)
        logits[...] += lax.dot_general(
            weight[:, columns], gathered[:, columns], (((1,), (1,)), ((), ())), preferred_element_type=F32
        )
        return carry

    lax.fori_loop(0, width // step, add_logits, 0)
    value = logits[...]
    top = jnp.max(value, axis=0, keepdims=True)
    hit = lax.broadcasted_iota(jnp.int32, (vocab_rows, resp), 0) == targets[...] - me * vocab_rows
    stat[...] = jnp.concatenate(
        [
            top,
            jnp.sum(jnp.exp(value - top), axis=0, keepdims=True),
            jnp.sum(jnp.where(hit, value, 0.0), axis=0, keepdims=True),
            jnp.zeros((5, resp), F32),
        ],
        axis=0,
    )
    stats[pl.ds(me, 1)] = stat[...][None]

    def send_stat(rel, carry):
        send(stat, stats.at[me], 3, device(rel))
        return carry

    lax.fori_loop(1, n, send_stat, 0)
    wait(recv_sems, 3, stats.at[pl.ds(0, n - 1)])
    tops = stats[:, 0, :]
    row_top = jnp.max(tops, axis=0, keepdims=True)
    row_total = jnp.sum(jnp.exp(tops - row_top) * stats[:, 1, :], axis=0, keepdims=True)
    target_logit = jnp.sum(stats[:, 2, :], axis=0, keepdims=True)
    log_prob = target_logit - row_top - jnp.log(row_total)
    sign = jnp.where(branch[...] == 1, 1.0, 0.0) - jnp.where(branch[...] == 2, 1.0, 0.0)
    pairs = pair_weight.shape[0]
    member = lax.broadcasted_iota(jnp.int32, (pairs, resp), 0) == pair_of_row[...]
    margin = jnp.sum(jnp.where(member, sign * (log_prob - ref_log_prob[...]), 0.0), axis=1, keepdims=True)
    z = -dpo_beta * margin
    softplus = jnp.maximum(z, 0.0) + jnp.log1p(jnp.exp(-jnp.abs(z)))
    loss[...] = jnp.sum(pair_weight[...] * softplus, axis=0, keepdims=True)
    push_back = pair_weight[...] * lax.logistic(z)
    row_scale = -dpo_beta * sign * jnp.sum(jnp.where(member, push_back, 0.0), axis=0, keepdims=True)
    probs = jnp.exp(value - row_top) / row_total
    rounded = (row_scale * (jnp.where(hit, 1.0, 0.0) - probs)).astype(BF16)
    dlogits[...] = rounded
    by_row = jnp.transpose(rounded.astype(F32)).astype(BF16)

    def add_partial(i, carry):
        columns = pl.ds(pl.multiple_of(i * step, step), step)
        partial[:, columns] = jnp.dot(by_row, weight[:, columns], preferred_element_type=F32)
        return carry

    lax.fori_loop(0, width // step, add_partial, 0)
    share = resp // seq
    for k in range(1, seq):
        peer = lax.rem(mine_seq + k, seq)
        rows = pl.ds(pl.multiple_of(peer * share, share), share)
        send(partial.at[rows], seq_parts.at[mine_seq], 4, (peer, mine_tensor))
    rows = pl.ds(pl.multiple_of(mine_seq * share, share), share)
    seq_parts[pl.ds(mine_seq, 1)] = partial[rows, :][None]
    wait(recv_sems, 4, seq_parts.at[pl.ds(0, seq - 1)])
    total = seq_parts[0]
    for k in range(1, seq):
        total = total + seq_parts[k]
    slab = sums.shape[2]
    cuts = [(i, i * slab, min((i + 1) * slab, width)) for i in range(tensor) if i * slab < width]
    sums[...] = jnp.zeros_like(sums)
    for i, low, high in cuts:
        sums[i, :, : high - low] = total[:, low:high]
    for k in range(1, tensor):
        peer = lax.rem(mine_tensor + k, tensor)
        send(sums.at[peer], tensor_parts.at[mine_tensor], 5, (mine_seq, peer))
    tensor_parts[pl.ds(mine_tensor, 1)] = sums[pl.ds(mine_tensor, 1)]
    wait(recv_sems, 5, tensor_parts.at[pl.ds(0, tensor - 1)])
    total = tensor_parts[0]
    for k in range(1, tensor):
        total = total + tensor_parts[k]
    done[...] = total
    pieces[pl.ds(mine_tensor, 1)] = total[None]
    for k in range(1, tensor):
        send(done, pieces.at[mine_tensor], 6, (mine_seq, lax.rem(mine_tensor + k, tensor)))
    wait(recv_sems, 6, pieces.at[pl.ds(0, tensor - 1)])
    for i, low, high in cuts:
        hidden_grad[:, low:high] = pieces[i, :, : high - low].astype(BF16)

    own.wait()
    others = pl.ds(ROWS, (n - 1) * ROWS)
    wait(recv_sems, 2, arrived_labels.at[others])
    wait(recv_sems, 1, arrived.at[others])
    wait(send_sems, 0, folded.at[pl.ds(0, (seq - 1) * ROWS)])
    wait(send_sems, 1, packed.at[others])
    wait(send_sems, 2, labels.at[others])
    wait(send_sems, 3, stats.at[pl.ds(0, n - 1)])
    wait(send_sems, 4, seq_parts.at[pl.ds(0, seq - 1)])
    wait(send_sems, 5, tensor_parts.at[pl.ds(0, tensor - 1)])
    wait(send_sems, 6, pieces.at[pl.ds(0, tensor - 1)])


def weight_grad_kernel(parts, subs, norm, arrived, labels, dlogits, gathered, out, tags, main_pick, rest):
    i = pl.program_id(0)
    vocab_rows, slots = main_pick.shape
    vocab = lax.broadcasted_iota(jnp.int32, (vocab_rows, slots), 0).astype(F32) + 1.0

    @pl.when(i == 0)
    def _():
        tags[...] = jnp.transpose(labels[...])
        main_pick[...] = jnp.where(vocab == tags[0:1, :], 1.0, 0.0).astype(BF16)
        rest[...] = jnp.zeros_like(rest)

    head = jnp.dot(dlogits[...], gathered[...], preferred_element_type=F32)
    sub = lax.rem(i, subs)

    @pl.when(i < parts * subs)
    def _():
        block = arrived[...]
        out[...] = (head + norm * jnp.dot(main_pick[...], block, preferred_element_type=F32)).astype(BF16)
        part = lax.div(i, subs)
        last_pick = jnp.where(vocab == tags[pl.ds(part + 1, 1), :], 1.0, 0.0).astype(BF16)
        rest[pl.ds(sub, 1)] += jnp.dot(last_pick, block, preferred_element_type=F32)[None]

    @pl.when(i >= parts * subs)
    def _():
        out[...] = (head + norm * rest[pl.ds(sub, 1)][0]).astype(BF16)


def shards(
    weight, hidden, targets, branch, pair_of_row, ref_log_prob, pair_weight, token_ids, token_grad
):
    vocab_rows, width = weight.shape
    seq, tensor = lax.axis_size("seq"), lax.axis_size("tensor")
    n = seq * tensor
    resp, tokens, pairs = targets.shape[0], token_ids.shape[0], pair_weight.shape[0]
    capacity = max(2, (2 * tokens + n - 1) // n)
    tiles = width // LANES
    piece, parts = pack_plan(capacity, tiles)
    subs = next(k for k in range(1, piece + 1) if piece % k == 0 and piece // k <= 8)
    block = piece // subs * LANES
    packed_width = parts * piece * LANES
    slab = (tiles + tensor - 1) // tensor * LANES
    half = width // 2
    folded = jnp.concatenate([hidden[:, :half], hidden[:, half:]], axis=0)
    vmem, hbm = pl.BlockSpec(memory_space=pltpu.VMEM), pl.BlockSpec(memory_space=pl.ANY)
    arrived, arrived_labels, dlogits, gathered, hidden_grad, loss = pl.pallas_call(
        functools.partial(exchange_kernel, seq, tensor, capacity, piece, parts),
        out_shape=(
            jax.ShapeDtypeStruct((n * ROWS, packed_width), BF16),
            jax.ShapeDtypeStruct((n * ROWS, LANES), F32),
            jax.ShapeDtypeStruct((vocab_rows, resp), BF16),
            jax.ShapeDtypeStruct((resp, width), BF16),
            jax.ShapeDtypeStruct(hidden.shape, BF16),
            jax.ShapeDtypeStruct((1, 1), F32),
        ),
        in_specs=[vmem] * 9 + [hbm],
        out_specs=(hbm, vmem, vmem, vmem, vmem, vmem),
        scratch_shapes=[
            pltpu.VMEM((vocab_rows, width), BF16),
            pltpu.VMEM((n * ROWS, packed_width), BF16),
            pltpu.VMEM((n * ROWS, LANES), F32),
            pltpu.VMEM((seq * ROWS, half), BF16),
            pltpu.VMEM((vocab_rows, resp), F32),
            pltpu.VMEM((8, resp), F32),
            pltpu.VMEM((n, 8, resp), F32),
            pltpu.VMEM((resp, width), F32),
            pltpu.VMEM((seq, resp // seq, width), F32),
            pltpu.VMEM((tensor, resp // seq, slab), F32),
            pltpu.VMEM((tensor, resp // seq, slab), F32),
            pltpu.VMEM((resp // seq, slab), F32),
            pltpu.VMEM((tensor, resp // seq, slab), F32),
            pltpu.SemaphoreType.DMA,
            pltpu.SemaphoreType.DMA,
            pltpu.SemaphoreType.DMA((7,)),
            pltpu.SemaphoreType.DMA((7,)),
        ],
        compiler_params=pltpu.CompilerParams(
            collective_id=0, has_side_effects=True, vmem_limit_bytes=60 << 20
        ),
        name="exchange",
    )(
        targets.reshape(1, resp),
        branch.reshape(1, resp),
        pair_of_row.reshape(1, resp),
        ref_log_prob.reshape(1, resp),
        pair_weight.reshape(pairs, 1),
        token_ids.reshape(1, tokens),
        token_ids.reshape(tokens, 1),
        folded,
        token_grad,
        weight,
    )
    last = parts * subs - 1
    weight_grad = pl.pallas_call(
        functools.partial(weight_grad_kernel, parts, subs, math.sqrt(width)),
        grid=((parts + 1) * subs,),
        out_shape=jax.ShapeDtypeStruct(weight.shape, BF16),
        in_specs=[
            pl.BlockSpec((n * ROWS, block), lambda i: (0, jnp.minimum(i, last))),
            pl.BlockSpec((n * ROWS, LANES), lambda i: (0, 0)),
            pl.BlockSpec((vocab_rows, resp), lambda i: (0, 0)),
            pl.BlockSpec((resp, block), lambda i: (0, i)),
        ],
        out_specs=pl.BlockSpec((vocab_rows, block), lambda i: (0, i)),
        scratch_shapes=[
            pltpu.VMEM((LANES, n * ROWS), F32),
            pltpu.VMEM((vocab_rows, n * ROWS), BF16),
            pltpu.VMEM((subs, vocab_rows, block), F32),
        ],
        compiler_params=pltpu.CompilerParams(vmem_limit_bytes=56 << 20),
        name="weight_grad",
    )(arrived, arrived_labels, dlogits, gathered)
    return (loss.reshape(()), weight_grad, hidden_grad)


def solution(mesh):
    return jax.shard_map(
        shards,
        mesh=mesh,
        in_specs=(
            P(("seq", "tensor"), None),
            P("seq", None),
            P(),
            P(),
            P(),
            P(),
            P(),
            P(("seq", "tensor")),
            P(("seq", "tensor"), None),
        ),
        out_specs=(P(), P(("seq", "tensor"), None), P("seq", None)),
        check_vma=False,
    )
```

time: 359 us -> 165 us (0.46)
  blocking collectives: 175 us -> 0 us
  Pallas kernels: 0 us -> 157 us
  waiting for transfers between devices: 84.5 us -> 0 us
  local copies, waits for them, and re-layouts: 39 us -> 4.22 us
  matrix products: 23.7 us -> 0 us
  starting transfers between devices: 19.5 us -> 0 us
  between operations: 14.1 us -> 2.42 us
    pallas_call x0 -> x2, Pallas kernels: none -> 157 us  [the longest x1 145 us: shards(): pl.pallas_call(functools.partial(exchange_kernel, seq, tensor, capacity,...]
    pmax x1 -> x0, blocking collectives: 103 us -> none  [shards(): row_top = lax.pmax(jnp.max(logits, axis=1), ('seq', 'tensor'))]
    psum x2 -> x0, blocking collectives: 62.7 us -> none  [the longest x1 39.6 us: shards(): lax.psum((jnp.sum(shifted, axis=1), target_part), ('seq', 'tensor'))]
    all_to_all x4 -> x0, waiting for transfers between devices: 52.3 us -> none  [the longest x1 51.5 us: shards(): lax.all_to_all(outgoing, 'seq', split_axis=0, concat_axis=0, tiled=True)]
    reduce_scatter x1 -> x0, waiting for transfers between devices: 32.2 us -> none  [shards(): lax.psum_scatter(jnp.dot(dlogits, weight, preferred_element_type=jnp.floa...]
    dot_general x4 -> x0, matrix products: 23.7 us -> none  [the longest x1 8.65 us: shards(): embed_grad = jnp.dot(onehot, arrived, preferred_element_type=jnp.float32)]
    all_to_all x4 -> x0, starting transfers between devices: 19.5 us -> none  [the longest x1 5.17 us: shards(): lax.all_to_all(labels, 'seq', split_axis=0, concat_axis=0, tiled=True)]
    reshape x4 -> x2, local copies, waits for them, and re-layouts: 19.3 us -> 2.77 us  [the longest x1 1.44 us: shards(): token_ids.reshape(tokens, 1)]
  transfers between devices with their start and end apart: 5 -> 0, of which waited for: 3 -> 0; matrix products, arithmetic and copies ran while one was open for 12% -> 0% of each run, Pallas kernels for 0% -> 0%
where the time goes in v1:
time: 165 us; the launch traced here: 164 us
  Pallas kernels  157 us (95%)
  local copies, waits for them, and re-layouts  4.22 us (3%)
  between operations  2.42 us (1%)
    pallas_call x1, Pallas kernels, shards(): pl.pallas_call(functools.partial(exchange_kernel, seq, tensor, capacity,...  145 us
    pallas_call x1, Pallas kernels, shards(): pl.pallas_call(functools.partial(weight_grad_kernel, parts, subs, math.sq...  11.9 us

profile of v1, /device:TPU:0, one launch (start us, length us, event | category | flops | bytes accessed | tf_op | source)
XLA Modules:
  0.0 164.2 jit_solution(9867564618248339345)
XLA Ops:
  0.6 1.3 copy.13.pair_weight
  2.0 0.8 fusion
  2.8 0.6 pad_maximum_fusion.hidden
  3.4 1.4 copy.14.ids_col
  4.9 145.0 %exchange.1 = (bf16[512,4480]{1,0:T(8,128)(2,1)}, f32[512,128]{1,0:T(8,128)}, bf16[512,64]{1,0:T(8,128)(2,1)}, bf16[64,5376]{1,0:T(8,128)(2,1)}, bf16[8,5376]{1,0:T(8,128)(2,1)}, /*index=5*/f32[1,1]{1,0:T(1,128)}) custom-call(s32[1,64]{1,0:T(1,128)} %bitcast.10, s32[1,64]{1,0:T(1,128)} %bitcast.11, s32[1,64]{1,0:T(1,128)} %bitcast.12, f32[1,64]{1,0:T(1,128)} %bitcast.13, ...), custom_call_target="tpu_custom_call" | custom-call | tf_op jit(solution)/shard_map/exchange/pallas_call | solution.py:284
  149.9 0.0 copy-start
  149.9 11.9 %weight_grad.1 = bf16[512,5376]{1,0:T(8,128)(2,1)} custom-call(bf16[512,4480]{1,0:T(8,128)(2,1)} %get-tuple-element.10.arrived, f32[512,128]{1,0:T(8,128)} %get-tuple-element.11.labels, bf16[512,64]{1,0:T(8,128)(2,1)} %get-tuple-element.12.dlogits, bf16[64,5376]{1,0:T(8,128)(2,1)} %get-tuple-element.13.gathered), custom_call_target="tpu_custom_call" | custom-call | tf_op jit(solution)/shard_map/weight_grad/pallas_call | solution.py:332
  162.4 0.0 copy-done
  162.4 0.6 copy.18
Async XLA Ops:
  149.9 12.5 %copy-start = (bf16[8,5376]{1,0:T(8,128)(2,1)S(1)}, bf16[8,5376]{1,0:T(8,128)(2,1)}, u32[]{:S(2)}) copy-start(bf16[8,5376]{1,0:T(8,128)(2,1)} %get-tuple-element.22) | copy-start | bytes 258052

commit v2 on v1

--- a/solution.py
+++ b/solution.py
@@ -12,6 +12,7 @@
 LANES = 128
 ROWS = 16
 CHUNK = 128
+WAVES = 4
 MESH = pl.DeviceIdType.MESH
 F32, BF16 = jnp.float32, jnp.bfloat16
 
@@ -123,7 +124,12 @@
         lax.fori_loop(0, CHUNK // ROWS, send_block, 0)
         return carry
 
-    lax.fori_loop(0, n * ROWS // CHUNK, pack, 0)
+    chunks = n * ROWS // CHUNK
+
+    def send_wave(wave):
+        lax.fori_loop(wave * chunks // WAVES, (wave + 1) * chunks // WAVES, pack, 0)
+
+    send_wave(0)
     own = pltpu.make_async_copy(packed.at[pl.ds(0, ROWS)], arrived.at[pl.ds(0, ROWS)], own_sem)
     own.start()
     arrived_labels[pl.ds(0, ROWS), :] = labels[pl.ds(0, ROWS), :]
@@ -166,6 +172,7 @@
         return carry
 
     lax.fori_loop(1, n, send_stat, 0)
+    send_wave(1)
     wait(recv_sems, 3, stats.at[pl.ds(0, n - 1)])
     tops = stats[:, 0, :]
     row_top = jnp.max(tops, axis=0, keepdims=True)
@@ -197,6 +204,7 @@
         peer = lax.rem(mine_seq + k, seq)
         rows = pl.ds(pl.multiple_of(peer * share, share), share)
         send(partial.at[rows], seq_parts.at[mine_seq], 4, (peer, mine_tensor))
+    send_wave(2)
     rows = pl.ds(pl.multiple_of(mine_seq * share, share), share)
     seq_parts[pl.ds(mine_seq, 1)] = partial[rows, :][None]
     wait(recv_sems, 4, seq_parts.at[pl.ds(0, seq - 1)])
@@ -211,6 +219,7 @@
     for k in range(1, tensor):
         peer = lax.rem(mine_tensor + k, tensor)
         send(sums.at[peer], tensor_parts.at[mine_tensor], 5, (mine_seq, peer))
+    send_wave(3)
     tensor_parts[pl.ds(mine_tensor, 1)] = sums[pl.ds(mine_tensor, 1)]
     wait(recv_sems, 5, tensor_parts.at[pl.ds(0, tensor - 1)])
     total = tensor_parts[0]

time: 165 us -> 162 us (0.982)
  the two profiles are of different devices: /device:TPU:0 before, /device:TPU:3 now
where the time goes in v2:
time: 162 us; the launch traced here: 161 us
  Pallas kernels  154 us (95%)
  local copies, waits for them, and re-layouts  4.22 us (3%)
  between operations  2.42 us (1%)
    pallas_call x1, Pallas kernels, shards(): pl.pallas_call(functools.partial(exchange_kernel, seq, tensor, capacity,...  142 us
    pallas_call x1, Pallas kernels, shards(): pl.pallas_call(functools.partial(weight_grad_kernel, parts, subs, math.sq...  11.9 us

profile of v2, /device:TPU:3, one launch (start us, length us, event | category | flops | bytes accessed | tf_op | source)
XLA Modules:
  0.0 161.4 jit_solution(7572737747533725256)
XLA Ops:
  0.6 1.3 copy.13.pair_weight
  2.0 0.8 fusion
  2.8 0.6 pad_maximum_fusion.hidden
  3.4 1.4 copy.14.ids_col
  4.9 142.2 %exchange.1 = (bf16[512,4480]{1,0:T(8,128)(2,1)}, f32[512,128]{1,0:T(8,128)}, bf16[512,64]{1,0:T(8,128)(2,1)}, bf16[64,5376]{1,0:T(8,128)(2,1)}, bf16[8,5376]{1,0:T(8,128)(2,1)}, /*index=5*/f32[1,1]{1,0:T(1,128)}) custom-call(s32[1,64]{1,0:T(1,128)} %bitcast.10, s32[1,64]{1,0:T(1,128)} %bitcast.11, s32[1,64]{1,0:T(1,128)} %bitcast.12, f32[1,64]{1,0:T(1,128)} %bitcast.13, ...), custom_call_target="tpu_custom_call" | custom-call | tf_op jit(solution)/shard_map/exchange/pallas_call | solution.py:293
  147.1 0.0 copy-start
  147.1 11.9 %weight_grad.1 = bf16[512,5376]{1,0:T(8,128)(2,1)} custom-call(bf16[512,4480]{1,0:T(8,128)(2,1)} %get-tuple-element.10.arrived, f32[512,128]{1,0:T(8,128)} %get-tuple-element.11.labels, bf16[512,64]{1,0:T(8,128)(2,1)} %get-tuple-element.12.dlogits, bf16[64,5376]{1,0:T(8,128)(2,1)} %get-tuple-element.13.gathered), custom_call_target="tpu_custom_call" | custom-call | tf_op jit(solution)/shard_map/weight_grad/pallas_call | solution.py:341
  159.6 0.0 copy-done
  159.6 0.6 copy.18
Async XLA Ops:
  147.1 12.5 %copy-start = (bf16[8,5376]{1,0:T(8,128)(2,1)S(1)}, bf16[8,5376]{1,0:T(8,128)(2,1)}, u32[]{:S(2)}) copy-start(bf16[8,5376]{1,0:T(8,128)(2,1)} %get-tuple-element.22) | copy-start | bytes 258052

commit v3 on v2

--- a/solution.py
+++ b/solution.py
@@ -12,6 +12,7 @@
 LANES = 128
 ROWS = 16
 CHUNK = 128
+TOKENS = 7
 WAVES = 4
 MESH = pl.DeviceIdType.MESH
 F32, BF16 = jnp.float32, jnp.bfloat16
@@ -26,11 +27,11 @@
 
 
 def exchange_kernel(
-    seq, tensor, capacity, piece, parts,
+    seq, tensor, capacity, piece, parts, block, early_waves, norm,
     targets, branch, pair_of_row, ref_log_prob, pair_weight, ids_row, ids_col, hidden, token_grad, weight_hbm,
-    arrived, arrived_labels, dlogits, gathered, hidden_grad, loss,
-    weight, packed, labels, folded, logits, stat, stats, partial, seq_parts, sums, tensor_parts, done, pieces,
-    load_sem, own_sem, send_sems, recv_sems,
+    arrived, base_hbm, tags, dlogits, gathered, hidden_grad, loss,
+    weight, packed, folded, logits, stat, stats, partial, seq_parts, sums, tensor_parts, done, pieces,
+    load_sem, own_sem, send_sems, recv_sems, *early_scratch,
 ):
     n = seq * tensor
     vocab_rows, width = weight.shape
@@ -79,6 +80,23 @@
     spare_row = rel_owner * ROWS + capacity + spare
     label = (ids_row[...] - owner * vocab_rows + 1).astype(F32)
     piece_width = piece * LANES
+    chunks = n * ROWS // CHUNK
+    wave_rows = n * ROWS // WAVES
+    if early_waves:
+        early, base, rest, base_sems = early_scratch
+
+    def exact_dot(left, right, dims):
+        high = left.astype(BF16)
+        low = (left - high.astype(F32)).astype(BF16)
+        ones = right.astype(BF16)
+        return lax.dot_general(high, ones, dims, preferred_element_type=F32) + lax.dot_general(
+            low, ones, dims, preferred_element_type=F32
+        )
+
+    to_rel = lax.broadcasted_iota(jnp.int32, (n, tokens), 0) == rel_owner
+    at_slot = jnp.where(lax.broadcasted_iota(jnp.int32, (resp, tokens), 0) == slot, 1.0, 0.0)
+    stat[...] = jnp.zeros_like(stat)
+    stat[:, 3, :] = exact_dot(jnp.where(to_rel, label, 0.0), at_slot, (((1,), (1,)), ((), ())))
 
     pl.semaphore_wait(barrier, n - 1)
 
@@ -87,52 +105,50 @@
     for k in range(1, seq):
         send(hidden, folded.at[mine_rows], 0, (lax.rem(mine_seq + k, seq), mine_tensor))
 
-    def pack(chunk, carry):
-        base = pl.multiple_of(chunk * CHUNK, CHUNK)
-        rows = base + lax.broadcasted_iota(jnp.int32, (CHUNK, tokens), 0)
-        lane = lax.broadcasted_iota(jnp.int32, (CHUNK, LANES), 1)
+    def pack(wave, chunk, carry):
+        first = pl.multiple_of(chunk * CHUNK, CHUNK)
+        rows = first + lax.broadcasted_iota(jnp.int32, (CHUNK, tokens), 0)
         main = rows == main_row
         in_spare = rows == spare_row
         main_pick = jnp.where(main, 1.0, 0.0).astype(BF16)
-        tags = jnp.where(lane == 0, jnp.sum(jnp.where(main, label, 0.0), axis=1, keepdims=True), 0.0)
         for part in range(parts):
             last = in_spare & (part_of == part)
             last_pick = jnp.where(last, 1.0, 0.0).astype(BF16)
-            tags = jnp.where(
-                lane == part + 1, jnp.sum(jnp.where(last, label, 0.0), axis=1, keepdims=True), tags
-            )
             here = pl.ds(part * piece_width, piece_width)
-            packed[pl.ds(base, CHUNK), here] = (
+            packed[pl.ds(first, CHUNK), here] = (
                 jnp.dot(main_pick, token_grad[:, here], preferred_element_type=F32)
                 + jnp.dot(
                     last_pick, token_grad[:, parts * piece_width :], preferred_element_type=F32
                 )
             ).astype(BF16)
-        labels[pl.ds(base, CHUNK), :] = tags
 
         def send_block(i, inner):
             rel = chunk * (CHUNK // ROWS) + i
-            block = pl.ds(pl.multiple_of(rel * ROWS, ROWS), ROWS)
+            src = pl.ds(pl.multiple_of(rel * ROWS, ROWS), ROWS)
+            if wave < early_waves:
+                land = early.at[src]
+            else:
+                land = arrived.at[pl.ds(pl.multiple_of(rel * ROWS - early_waves * wave_rows, ROWS), ROWS)]
 
             @pl.when(rel > 0)
             def _():
-                send(packed.at[block], arrived.at[block], 1, device(rel))
-                send(labels.at[block], arrived_labels.at[block], 2, device(rel))
+                send(packed.at[src], land, TOKENS + wave, device(rel))
 
             return inner
 
         lax.fori_loop(0, CHUNK // ROWS, send_block, 0)
         return carry
 
-    chunks = n * ROWS // CHUNK
-
     def send_wave(wave):
-        lax.fori_loop(wave * chunks // WAVES, (wave + 1) * chunks // WAVES, pack, 0)
+        lax.fori_loop(
+            wave * chunks // WAVES, (wave + 1) * chunks // WAVES, functools.partial(pack, wave), 0
+        )
 
     send_wave(0)
-    own = pltpu.make_async_copy(packed.at[pl.ds(0, ROWS)], arrived.at[pl.ds(0, ROWS)], own_sem)
+    own = pltpu.make_async_copy(
+        packed.at[pl.ds(0, ROWS)], (early if early_waves else arrived).at[pl.ds(0, ROWS)], own_sem
+    )
     own.start()
-    arrived_labels[pl.ds(0, ROWS), :] = labels[pl.ds(0, ROWS), :]
 
     wait(recv_sems, 0, folded.at[pl.ds(0, (seq - 1) * ROWS)])
     half = width // 2
@@ -156,19 +172,13 @@
     value = logits[...]
     top = jnp.max(value, axis=0, keepdims=True)
     hit = lax.broadcasted_iota(jnp.int32, (vocab_rows, resp), 0) == targets[...] - me * vocab_rows
-    stat[...] = jnp.concatenate(
-        [
-            top,
-            jnp.sum(jnp.exp(value - top), axis=0, keepdims=True),
-            jnp.sum(jnp.where(hit, value, 0.0), axis=0, keepdims=True),
-            jnp.zeros((5, resp), F32),
-        ],
-        axis=0,
-    )
-    stats[pl.ds(me, 1)] = stat[...][None]
+    stat[:, 0, :] = jnp.broadcast_to(top, (n, resp))
+    stat[:, 1, :] = jnp.broadcast_to(jnp.sum(jnp.exp(value - top), axis=0, keepdims=True), (n, resp))
+    stat[:, 2, :] = jnp.broadcast_to(jnp.sum(jnp.where(hit, value, 0.0), axis=0, keepdims=True), (n, resp))
+    stats[pl.ds(me, 1)] = stat[pl.ds(0, 1)]
 
     def send_stat(rel, carry):
-        send(stat, stats.at[me], 3, device(rel))
+        send(stat.at[rel], stats.at[me], 3, device(rel))
         return carry
 
     lax.fori_loop(1, n, send_stat, 0)
@@ -233,44 +243,92 @@
     for i, low, high in cuts:
         hidden_grad[:, low:high] = pieces[i, :, : high - low].astype(BF16)
 
+    slots = n * ROWS
+    column = lax.broadcasted_iota(jnp.int32, (resp, slots), 1)
+    column = column - jnp.right_shift(column, ROWS.bit_length() - 1) * ROWS
+    wanted = lax.broadcasted_iota(jnp.int32, (resp, slots), 0)
+    came = lax.broadcasted_iota(jnp.int32, (n, slots), 1)
+    came = me - jnp.right_shift(came, ROWS.bit_length() - 1)
+    came = jnp.where(came < 0, came + n, came) == lax.broadcasted_iota(jnp.int32, (n, slots), 0)
+    sent_labels = stats[:, 3, :]
+    tags[...] = jnp.zeros_like(tags)
+    for k in range(parts + 1):
+        if k == 0:
+            chosen = (column == wanted) & (column < capacity)
+        else:
+            chosen = (column >= capacity) & (wanted == (column - capacity) * parts + (k - 1))
+        spread = exact_dot(sent_labels, jnp.where(chosen, 1.0, 0.0), (((1,), (0,)), ((), ())))
+        tags[k : k + 1, :] = jnp.sum(jnp.where(came, spread, 0.0), axis=0, keepdims=True)
+
     own.wait()
-    others = pl.ds(ROWS, (n - 1) * ROWS)
-    wait(recv_sems, 2, arrived_labels.at[others])
-    wait(recv_sems, 1, arrived.at[others])
+
+    def wait_wave(wave):
+        low, high = wave * wave_rows + (ROWS if wave == 0 else 0), (wave + 1) * wave_rows
+        wait(send_sems, TOKENS + wave, packed.at[pl.ds(low, high - low)])
+        if wave < early_waves:
+            wait(recv_sems, TOKENS + wave, early.at[pl.ds(low, high - low)])
+        else:
+            wait(recv_sems, TOKENS + wave, arrived.at[pl.ds(low - early_waves * wave_rows, high - low)])
+
+    if early_waves:
+        for wave in range(early_waves):
+            wait_wave(wave)
+        count = early_waves * wave_rows
+        vocab = lax.broadcasted_iota(jnp.int32, (vocab_rows, count), 0).astype(F32) + 1.0
+        main_pick = jnp.where(vocab == tags[0:1, :count], 1.0, 0.0).astype(BF16)
+        subs = piece_width // block
+        rest[...] = jnp.zeros_like(rest)
+        stores = []
+        for i in range((parts + 1) * subs):
+            here = pl.ds(i * block, block)
+            head = jnp.dot(dlogits[...], gathered[:, here], preferred_element_type=F32)
+            if i < parts * subs:
+                part = i // subs
+                last_pick = jnp.where(vocab == tags[part + 1 : part + 2, :count], 1.0, 0.0).astype(BF16)
+                base[i] = head + norm * jnp.dot(main_pick, early[:, here], preferred_element_type=F32)
+                rest[i % subs] += jnp.dot(last_pick, early[:, here], preferred_element_type=F32)
+            else:
+                base[i] = head + norm * rest[i % subs]
+            stores.append(pltpu.make_async_copy(base.at[i], base_hbm.at[i], base_sems.at[i]))
+            stores[-1].start()
+        for store in stores:
+            store.wait()
+    for wave in range(early_waves, WAVES):
+        wait_wave(wave)
     wait(send_sems, 0, folded.at[pl.ds(0, (seq - 1) * ROWS)])
-    wait(send_sems, 1, packed.at[others])
-    wait(send_sems, 2, labels.at[others])
     wait(send_sems, 3, stats.at[pl.ds(0, n - 1)])
     wait(send_sems, 4, seq_parts.at[pl.ds(0, seq - 1)])
     wait(send_sems, 5, tensor_parts.at[pl.ds(0, tensor - 1)])
     wait(send_sems, 6, pieces.at[pl.ds(0, tensor - 1)])
 
 
-def weight_grad_kernel(parts, subs, norm, arrived, labels, dlogits, gathered, out, tags, main_pick, rest):
+def weight_grad_kernel(parts, subs, skipped, norm, arrived, tags, dlogits, gathered, base, out, main_pick, rest):
     i = pl.program_id(0)
     vocab_rows, slots = main_pick.shape
     vocab = lax.broadcasted_iota(jnp.int32, (vocab_rows, slots), 0).astype(F32) + 1.0
 
     @pl.when(i == 0)
     def _():
-        tags[...] = jnp.transpose(labels[...])
-        main_pick[...] = jnp.where(vocab == tags[0:1, :], 1.0, 0.0).astype(BF16)
+        main_pick[...] = jnp.where(vocab == tags[0:1, skipped:], 1.0, 0.0).astype(BF16)
         rest[...] = jnp.zeros_like(rest)
 
-    head = jnp.dot(dlogits[...], gathered[...], preferred_element_type=F32)
+    if skipped:
+        before = base[0]
+    else:
+        before = jnp.dot(dlogits[...], gathered[...], preferred_element_type=F32)
     sub = lax.rem(i, subs)
 
     @pl.when(i < parts * subs)
     def _():
         block = arrived[...]
-        out[...] = (head + norm * jnp.dot(main_pick[...], block, preferred_element_type=F32)).astype(BF16)
+        out[...] = (before + norm * jnp.dot(main_pick[...], block, preferred_element_type=F32)).astype(BF16)
         part = lax.div(i, subs)
-        last_pick = jnp.where(vocab == tags[pl.ds(part + 1, 1), :], 1.0, 0.0).astype(BF16)
+        last_pick = jnp.where(vocab == tags[pl.ds(part + 1, 1), :][:, skipped:], 1.0, 0.0).astype(BF16)
         rest[pl.ds(sub, 1)] += jnp.dot(last_pick, block, preferred_element_type=F32)[None]
 
     @pl.when(i >= parts * subs)
     def _():
-        out[...] = (head + norm * rest[pl.ds(sub, 1)][0]).astype(BF16)
+        out[...] = (before + norm * rest[pl.ds(sub, 1)][0]).astype(BF16)
 
 
 def shards(
@@ -290,25 +348,37 @@
     half = width // 2
     folded = jnp.concatenate([hidden[:, :half], hidden[:, half:]], axis=0)
     vmem, hbm = pl.BlockSpec(memory_space=pltpu.VMEM), pl.BlockSpec(memory_space=pl.ANY)
-    arrived, arrived_labels, dlogits, gathered, hidden_grad, loss = pl.pallas_call(
-        functools.partial(exchange_kernel, seq, tensor, capacity, piece, parts),
+    norm = math.sqrt(width)
+    slots = n * ROWS
+    early_waves = WAVES - 1 if slots * packed_width * 2 <= 8 << 20 else 0
+    skipped = early_waves * slots // WAVES
+    steps = (parts + 1) * subs
+    base_shape = (steps, vocab_rows, block) if early_waves else (1, 8, LANES)
+    early_scratch = [
+        pltpu.VMEM((skipped, packed_width), BF16),
+        pltpu.VMEM(base_shape, F32),
+        pltpu.VMEM((subs, vocab_rows, block), F32),
+        pltpu.SemaphoreType.DMA((steps,)),
+    ]
+    arrived, base, tags, dlogits, gathered, hidden_grad, loss = pl.pallas_call(
+        functools.partial(exchange_kernel, seq, tensor, capacity, piece, parts, block, early_waves, norm),
         out_shape=(
-            jax.ShapeDtypeStruct((n * ROWS, packed_width), BF16),
-            jax.ShapeDtypeStruct((n * ROWS, LANES), F32),
+            jax.ShapeDtypeStruct((slots - skipped, packed_width), BF16),
+            jax.ShapeDtypeStruct(base_shape, F32),
+            jax.ShapeDtypeStruct((8, slots), F32),
             jax.ShapeDtypeStruct((vocab_rows, resp), BF16),
             jax.ShapeDtypeStruct((resp, width), BF16),
             jax.ShapeDtypeStruct(hidden.shape, BF16),
             jax.ShapeDtypeStruct((1, 1), F32),
         ),
         in_specs=[vmem] * 9 + [hbm],
-        out_specs=(hbm, vmem, vmem, vmem, vmem, vmem),
+        out_specs=(hbm, hbm, vmem, vmem, vmem, vmem, vmem),
         scratch_shapes=[
             pltpu.VMEM((vocab_rows, width), BF16),
-            pltpu.VMEM((n * ROWS, packed_width), BF16),
-            pltpu.VMEM((n * ROWS, LANES), F32),
+            pltpu.VMEM((slots, packed_width), BF16),
             pltpu.VMEM((seq * ROWS, half), BF16),
             pltpu.VMEM((vocab_rows, resp), F32),
-            pltpu.VMEM((8, resp), F32),
+            pltpu.VMEM((n, 8, resp), F32),
             pltpu.VMEM((n, 8, resp), F32),
             pltpu.VMEM((resp, width), F32),
             pltpu.VMEM((seq, resp // seq, width), F32),
@@ -318,9 +388,10 @@
             pltpu.VMEM((tensor, resp // seq, slab), F32),
             pltpu.SemaphoreType.DMA,
             pltpu.SemaphoreType.DMA,
-            pltpu.SemaphoreType.DMA((7,)),
-            pltpu.SemaphoreType.DMA((7,)),
-        ],
+            pltpu.SemaphoreType.DMA((TOKENS + WAVES,)),
+            pltpu.SemaphoreType.DMA((TOKENS + WAVES,)),
+        ]
+        + (early_scratch if early_waves else []),
         compiler_params=pltpu.CompilerParams(
             collective_id=0, has_side_effects=True, vmem_limit_bytes=60 << 20
         ),
@@ -339,24 +410,24 @@
     )
     last = parts * subs - 1
     weight_grad = pl.pallas_call(
-        functools.partial(weight_grad_kernel, parts, subs, math.sqrt(width)),
-        grid=((parts + 1) * subs,),
+        functools.partial(weight_grad_kernel, parts, subs, skipped, norm),
+        grid=(steps,),
         out_shape=jax.ShapeDtypeStruct(weight.shape, BF16),
         in_specs=[
-            pl.BlockSpec((n * ROWS, block), lambda i: (0, jnp.minimum(i, last))),
-            pl.BlockSpec((n * ROWS, LANES), lambda i: (0, 0)),
+            pl.BlockSpec((slots - skipped, block), lambda i: (0, jnp.minimum(i, last))),
+            pl.BlockSpec((8, slots), lambda i: (0, 0)),
             pl.BlockSpec((vocab_rows, resp), lambda i: (0, 0)),
             pl.BlockSpec((resp, block), lambda i: (0, i)),
+            pl.BlockSpec((1,) + base_shape[1:], lambda i: (jnp.minimum(i, base_shape[0] - 1), 0, 0)),
         ],
         out_specs=pl.BlockSpec((vocab_rows, block), lambda i: (0, i)),
         scratch_shapes=[
-            pltpu.VMEM((LANES, n * ROWS), F32),
-            pltpu.VMEM((vocab_rows, n * ROWS), BF16),
+            pltpu.VMEM((vocab_rows, slots - skipped), BF16),
             pltpu.VMEM((subs, vocab_rows, block), F32),
         ],
         compiler_params=pltpu.CompilerParams(vmem_limit_bytes=56 << 20),
         name="weight_grad",
-    )(arrived, arrived_labels, dlogits, gathered)
+    )(arrived, tags, dlogits, gathered, base)
     return (loss.reshape(()), weight_grad, hidden_grad)
 
 

time: 162 us -> 167 us (1.031)
  the two profiles are of different devices: /device:TPU:3 before, /device:TPU:7 now
where the time goes in v3:
time: 167 us; the launch traced here: 166 us
  Pallas kernels  159 us (95%)
  local copies, waits for them, and re-layouts  4.22 us (3%)
  between operations  2.41 us (1%)
    pallas_call x1, Pallas kernels, shards(): pl.pallas_call(functools.partial(exchange_kernel, seq, tensor, capacity,...  149 us
    pallas_call x1, Pallas kernels, shards(): pl.pallas_call(functools.partial(weight_grad_kernel, parts, subs, skipped...  10.2 us

profile of v3, /device:TPU:7, one launch (start us, length us, event | category | flops | bytes accessed | tf_op | source)
XLA Modules:
  0.0 166.5 jit_solution(2836342716639681111)
XLA Ops:
  0.6 1.3 copy.13.pair_weight
  2.0 0.8 fusion
  2.8 0.6 pad_maximum_fusion.hidden
  3.4 1.4 copy.14.ids_col
  4.9 149.0 %exchange.1 = (bf16[128,4480]{1,0:T(8,128)(2,1)}, f32[6,512,896]{2,1,0:T(8,128)}, f32[8,512]{1,0:T(8,128)}, bf16[512,64]{1,0:T(8,128)(2,1)}, bf16[64,5376]{1,0:T...) custom-call(s32[1,64]{1,0:T(1,128)} %bitcast.10, s32[1,64]{1,0:T(1,128)} %bitcast.11, s32[1,64]{1,0:T(1,128)} %bitcast.12, ...), custom_call_target="tpu_custom_call" | custom-call | tf_op jit(solution)/shard_map/exchange/pallas_call | solution.py:363
  153.8 0.0 copy-start
  153.8 10.2 %weight_grad.1 = bf16[512,5376]{1,0:T(8,128)(2,1)} custom-call(bf16[128,4480]{1,0:T(8,128)(2,1)} %get-tuple-element.11.arrived, f32[8,512]{1,0:T(8,128)} %get-tuple-element.12.tags, bf16[512,64]{1,0:T(8,128)(2,1)} %get-tuple-element.13.dlogits, bf16[64,5376]{1,0:T(8,128)(2,1)} %get-tuple-element.14.gathered, f32[6,512,896]{2,1,0:T(8,128)} %get-tuple-element.15.base), custom_call_target="tpu_custom_call" | custom-call | tf_op jit(solution)/shard_map/weight_grad/pallas_call | solution.py:412
  164.7 0.0 copy-done
  164.7 0.6 copy.18
Async XLA Ops:
  153.8 10.9 %copy-start = (bf16[8,5376]{1,0:T(8,128)(2,1)S(1)}, bf16[8,5376]{1,0:T(8,128)(2,1)}, u32[]{:S(2)}) copy-start(bf16[8,5376]{1,0:T(8,128)(2,1)} %get-tuple-element.24) | copy-start | bytes 258052

commit v4 on v3

--- a/solution.py
+++ b/solution.py
@@ -40,9 +40,23 @@
     mine_seq, mine_tensor = lax.axis_index("seq"), lax.axis_index("tensor")
     me = mine_seq * tensor + mine_tensor
 
-    def device(rel):
-        peer = lax.rem(me + rel, n)
-        return (lax.div(peer, tensor), lax.rem(peer, tensor))
+    core = lax.rem(mine_seq, 2)
+
+    def exclusive_or(a, b, size):
+        total = 0
+        for bit in [1 << k for k in range(size.bit_length() - 1)]:
+            total = total + lax.rem(lax.div(a, bit) + lax.div(b, bit), 2) * bit
+        return total
+
+    own_block = 1 - core
+
+    def device(b):
+        place = lax.rem(b, tensor)
+        bits = lax.rem(place + 1 + core, 2) * (tensor // 2) + lax.div(place, 2)
+        return (
+            exclusive_or(mine_seq, lax.div(b, tensor), seq),
+            exclusive_or(mine_tensor, bits, tensor),
+        )
 
     def send(src, dst, kind, target):
         pltpu.make_async_remote_copy(
@@ -58,7 +72,10 @@
     barrier = pltpu.get_barrier_semaphore()
 
     def greet(rel, carry):
-        pl.semaphore_signal(barrier, inc=1, device_id=device(rel), device_id_type=MESH)
+        peer = lax.rem(me + rel, n)
+        pl.semaphore_signal(
+            barrier, inc=1, device_id=(lax.div(peer, tensor), lax.rem(peer, tensor)), device_id_type=MESH
+        )
         return carry
 
     lax.fori_loop(1, n, greet, 0)
@@ -70,8 +87,10 @@
         jnp.int32, (tokens, tokens), 1
     )
     slot = jnp.sum(jnp.where((owner_col == owner) & before, 1.0, 0.0), axis=0, keepdims=True).astype(jnp.int32)
-    rel_owner = owner - me
-    rel_owner = jnp.where(rel_owner < 0, rel_owner + n, rel_owner)
+    seq_bits = jnp.right_shift(owner, tensor.bit_length() - 1) ^ mine_seq
+    tensor_bits = (owner & (tensor - 1)) ^ mine_tensor
+    crosses = jnp.where(tensor_bits >= tensor // 2, 1, 0)
+    rel_owner = seq_bits * tensor + (tensor_bits & (tensor // 2 - 1)) * 2 + ((crosses + 1 + core) & 1)
     spare = jnp.zeros_like(slot)
     for j in range(1, ROWS - capacity):
         spare = spare + jnp.where(slot >= j * parts, 1, 0)
@@ -122,32 +141,34 @@
                 )
             ).astype(BF16)
 
-        def send_block(i, inner):
-            rel = chunk * (CHUNK // ROWS) + i
-            src = pl.ds(pl.multiple_of(rel * ROWS, ROWS), ROWS)
-            if wave < early_waves:
-                land = early.at[src]
-            else:
-                land = arrived.at[pl.ds(pl.multiple_of(rel * ROWS - early_waves * wave_rows, ROWS), ROWS)]
-
-            @pl.when(rel > 0)
-            def _():
-                send(packed.at[src], land, TOKENS + wave, device(rel))
-
-            return inner
-
-        lax.fori_loop(0, CHUNK // ROWS, send_block, 0)
         return carry
 
-    def send_wave(wave):
-        lax.fori_loop(
-            wave * chunks // WAVES, (wave + 1) * chunks // WAVES, functools.partial(pack, wave), 0
-        )
-
-    send_wave(0)
-    own = pltpu.make_async_copy(
-        packed.at[pl.ds(0, ROWS)], (early if early_waves else arrived).at[pl.ds(0, ROWS)], own_sem
-    )
+    def pack_wave(wave):
+        lax.fori_loop(wave * chunks // WAVES, (wave + 1) * chunks // WAVES, functools.partial(pack, wave), 0)
+
+    def send_blocks(first_eighth, end_eighth):
+        for eighth in range(first_eighth, end_eighth):
+            wave = eighth * WAVES // 8
+
+            def send_block(b, carry):
+                src = pl.ds(pl.multiple_of(b * ROWS, ROWS), ROWS)
+                if wave < early_waves:
+                    land = early.at[src]
+                else:
+                    land = arrived.at[pl.ds(pl.multiple_of(b * ROWS - early_waves * wave_rows, ROWS), ROWS)]
+
+                @pl.when(b != own_block)
+                def _():
+                    send(packed.at[src], land, TOKENS + wave, device(b))
+
+                return carry
+
+            lax.fori_loop(eighth * n // 8, (eighth + 1) * n // 8, send_block, 0)
+
+    pack_wave(0)
+    send_blocks(0, 1)
+    own_rows = pl.ds(pl.multiple_of(own_block * ROWS, ROWS), ROWS)
+    own = pltpu.make_async_copy(packed.at[own_rows], (early if early_waves else arrived).at[own_rows], own_sem)
     own.start()
 
     wait(recv_sems, 0, folded.at[pl.ds(0, (seq - 1) * ROWS)])
@@ -175,14 +196,18 @@
     stat[:, 0, :] = jnp.broadcast_to(top, (n, resp))
     stat[:, 1, :] = jnp.broadcast_to(jnp.sum(jnp.exp(value - top), axis=0, keepdims=True), (n, resp))
     stat[:, 2, :] = jnp.broadcast_to(jnp.sum(jnp.where(hit, value, 0.0), axis=0, keepdims=True), (n, resp))
-    stats[pl.ds(me, 1)] = stat[pl.ds(0, 1)]
+    stats[pl.ds(me, 1)] = stat[pl.ds(own_block, 1)]
 
     def send_stat(rel, carry):
-        send(stat.at[rel], stats.at[me], 3, device(rel))
+        @pl.when(rel != own_block)
+        def _():
+            send(stat.at[rel], stats.at[me], 3, device(rel))
+
         return carry
 
-    lax.fori_loop(1, n, send_stat, 0)
-    send_wave(1)
+    lax.fori_loop(0, n, send_stat, 0)
+    send_blocks(1, 2)
+    pack_wave(1)
     wait(recv_sems, 3, stats.at[pl.ds(0, n - 1)])
     tops = stats[:, 0, :]
     row_top = jnp.max(tops, axis=0, keepdims=True)
@@ -214,7 +239,8 @@
         peer = lax.rem(mine_seq + k, seq)
         rows = pl.ds(pl.multiple_of(peer * share, share), share)
         send(partial.at[rows], seq_parts.at[mine_seq], 4, (peer, mine_tensor))
-    send_wave(2)
+    send_blocks(2, 4)
+    pack_wave(2)
     rows = pl.ds(pl.multiple_of(mine_seq * share, share), share)
     seq_parts[pl.ds(mine_seq, 1)] = partial[rows, :][None]
     wait(recv_sems, 4, seq_parts.at[pl.ds(0, seq - 1)])
@@ -229,7 +255,8 @@
     for k in range(1, tensor):
         peer = lax.rem(mine_tensor + k, tensor)
         send(sums.at[peer], tensor_parts.at[mine_tensor], 5, (mine_seq, peer))
-    send_wave(3)
+    send_blocks(4, 5)
+    pack_wave(3)
     tensor_parts[pl.ds(mine_tensor, 1)] = sums[pl.ds(mine_tensor, 1)]
     wait(recv_sems, 5, tensor_parts.at[pl.ds(0, tensor - 1)])
     total = tensor_parts[0]
@@ -239,17 +266,20 @@
     pieces[pl.ds(mine_tensor, 1)] = total[None]
     for k in range(1, tensor):
         send(done, pieces.at[mine_tensor], 6, (mine_seq, lax.rem(mine_tensor + k, tensor)))
-    wait(recv_sems, 6, pieces.at[pl.ds(0, tensor - 1)])
-    for i, low, high in cuts:
-        hidden_grad[:, low:high] = pieces[i, :, : high - low].astype(BF16)
+    send_blocks(5, 8)
 
     slots = n * ROWS
     column = lax.broadcasted_iota(jnp.int32, (resp, slots), 1)
     column = column - jnp.right_shift(column, ROWS.bit_length() - 1) * ROWS
     wanted = lax.broadcasted_iota(jnp.int32, (resp, slots), 0)
     came = lax.broadcasted_iota(jnp.int32, (n, slots), 1)
-    came = me - jnp.right_shift(came, ROWS.bit_length() - 1)
-    came = jnp.where(came < 0, came + n, came) == lax.broadcasted_iota(jnp.int32, (n, slots), 0)
+    came = jnp.right_shift(came, ROWS.bit_length() - 1)
+    place = came & (tensor - 1)
+    seq_bits = jnp.right_shift(came, tensor.bit_length() - 1)
+    crosses = (place + 1 + ((seq_bits + core) & 1)) & 1
+    tensor_bits = crosses * (tensor // 2) + jnp.right_shift(place, 1)
+    came = (seq_bits ^ mine_seq) * tensor + (tensor_bits ^ mine_tensor)
+    came = came == lax.broadcasted_iota(jnp.int32, (n, slots), 0)
     sent_labels = stats[:, 3, :]
     tags[...] = jnp.zeros_like(tags)
     for k in range(parts + 1):
@@ -293,6 +323,10 @@
             stores[-1].start()
         for store in stores:
             store.wait()
+    wait(recv_sems, 6, pieces.at[pl.ds(0, tensor - 1)])
+    for i, low, high in cuts:
+        hidden_grad[:, low:high] = pieces[i, :, : high - low].astype(BF16)
+
     for wave in range(early_waves, WAVES):
         wait_wave(wave)
     wait(send_sems, 0, folded.at[pl.ds(0, (seq - 1) * ROWS)])

time: 167 us -> 146 us (0.87)
  the two profiles are of different devices: /device:TPU:7 before, /device:TPU:0 now
where the time goes in v4:
time: 146 us; the launch traced here: 145 us
  Pallas kernels  137 us (94%)
  local copies, waits for them, and re-layouts  4.22 us (3%)
  between operations  2.41 us (2%)
    pallas_call x1, Pallas kernels, shards(): pl.pallas_call(functools.partial(exchange_kernel, seq, tensor, capacity,...  127 us
    pallas_call x1, Pallas kernels, shards(): pl.pallas_call(functools.partial(weight_grad_kernel, parts, subs, skipped...  10.2 us

profile of v4, /device:TPU:0, one launch (start us, length us, event | category | flops | bytes accessed | tf_op | source)
XLA Modules:
  0.0 144.6 jit_solution(8618388189517118488)
XLA Ops:
  0.6 1.3 copy.13.pair_weight
  2.0 0.8 fusion
  2.8 0.6 pad_maximum_fusion.hidden
  3.4 1.4 copy.14.ids_col
  4.9 127.1 %exchange.1 = (bf16[128,4480]{1,0:T(8,128)(2,1)}, f32[6,512,896]{2,1,0:T(8,128)}, f32[8,512]{1,0:T(8,128)}, bf16[512,64]{1,0:T(8,128)(2,1)}, bf16[64,5376]{1,0:T...) custom-call(s32[1,64]{1,0:T(1,128)} %bitcast.10, s32[1,64]{1,0:T(1,128)} %bitcast.11, s32[1,64]{1,0:T(1,128)} %bitcast.12, ...), custom_call_target="tpu_custom_call" | custom-call | tf_op jit(solution)/shard_map/exchange/pallas_call | solution.py:397
  131.9 0.0 copy-start
  131.9 10.2 %weight_grad.1 = bf16[512,5376]{1,0:T(8,128)(2,1)} custom-call(bf16[128,4480]{1,0:T(8,128)(2,1)} %get-tuple-element.11.arrived, f32[8,512]{1,0:T(8,128)} %get-tuple-element.12.tags, bf16[512,64]{1,0:T(8,128)(2,1)} %get-tuple-element.13.dlogits, bf16[64,5376]{1,0:T(8,128)(2,1)} %get-tuple-element.14.gathered, f32[6,512,896]{2,1,0:T(8,128)} %get-tuple-element.15.base), custom_call_target="tpu_custom_call" | custom-call | tf_op jit(solution)/shard_map/weight_grad/pallas_call | solution.py:446
  142.8 0.0 copy-done
  142.8 0.6 copy.18
Async XLA Ops:
  131.9 10.9 %copy-start = (bf16[8,5376]{1,0:T(8,128)(2,1)S(1)}, bf16[8,5376]{1,0:T(8,128)(2,1)}, u32[]{:S(2)}) copy-start(bf16[8,5376]{1,0:T(8,128)(2,1)} %get-tuple-element.24) | copy-start | bytes 258052

commit v5 on v4

--- a/solution.py
+++ b/solution.py
@@ -26,11 +26,24 @@
     raise ValueError("no packing")
 
 
+def unpack_pick(capacity, parts, part):
+    to = lax.broadcasted_iota(jnp.int32, (CHUNK, CHUNK), 0)
+    source = lax.broadcasted_iota(jnp.int32, (CHUNK, CHUNK), 1)
+    bits = ROWS.bit_length() - 1
+    spare = (source & (ROWS - 1)) - capacity
+    chosen = (
+        (jnp.right_shift(to, bits) == jnp.right_shift(source, bits))
+        & (spare >= 0)
+        & ((to & (ROWS - 1)) == spare * parts + part)
+    )
+    return jnp.where(chosen, 1.0, 0.0).astype(BF16)
+
+
 def exchange_kernel(
     seq, tensor, capacity, piece, parts, block, early_waves, norm,
-    targets, branch, pair_of_row, ref_log_prob, pair_weight, ids_row, ids_col, hidden, token_grad, weight_hbm,
+    targets, branch, pair_of_row, ref_log_prob, pair_weight_row, ids_row, hidden_rows, token_grad, weight_hbm,
     arrived, base_hbm, tags, dlogits, gathered, hidden_grad, loss,
-    weight, packed, folded, logits, stat, stats, partial, seq_parts, sums, tensor_parts, done, pieces,
+    weight, packed, hidden, folded, logits, stat, stats, partial, seq_parts, sums, tensor_parts, done, pieces,
     load_sem, own_sem, send_sems, recv_sems, *early_scratch,
 ):
     n = seq * tensor
@@ -69,6 +82,10 @@
 
     load = pltpu.make_async_copy(weight_hbm, weight, load_sem)
     load.start()
+    half = width // 2
+    whole = hidden_rows[...].astype(F32)
+    hidden[...] = jnp.concatenate([whole[:, :half], whole[:, half:]], axis=0).astype(BF16)
+    folded[pl.ds(pl.multiple_of(mine_seq * ROWS, ROWS), ROWS)] = hidden[...]
     barrier = pltpu.get_barrier_semaphore()
 
     def greet(rel, carry):
@@ -82,11 +99,16 @@
 
     shift = vocab_rows.bit_length() - 1
     owner = jnp.right_shift(ids_row[...], shift)
-    owner_col = jnp.right_shift(ids_col[...], shift)
     before = lax.broadcasted_iota(jnp.int32, (tokens, tokens), 0) < lax.broadcasted_iota(
         jnp.int32, (tokens, tokens), 1
     )
-    slot = jnp.sum(jnp.where((owner_col == owner) & before, 1.0, 0.0), axis=0, keepdims=True).astype(jnp.int32)
+    to_owner = lax.broadcasted_iota(jnp.int32, (n, tokens), 0) == owner
+    earlier = jnp.dot(
+        jnp.where(to_owner, 1.0, 0.0).astype(BF16),
+        jnp.where(before, 1.0, 0.0).astype(BF16),
+        preferred_element_type=F32,
+    )
+    slot = jnp.sum(jnp.where(to_owner, earlier, 0.0), axis=0, keepdims=True).astype(jnp.int32)
     seq_bits = jnp.right_shift(owner, tensor.bit_length() - 1) ^ mine_seq
     tensor_bits = (owner & (tensor - 1)) ^ mine_tensor
     crosses = jnp.where(tensor_bits >= tensor // 2, 1, 0)
@@ -120,7 +142,6 @@
     pl.semaphore_wait(barrier, n - 1)
 
     mine_rows = pl.ds(pl.multiple_of(mine_seq * ROWS, ROWS), ROWS)
-    folded[mine_rows] = hidden[...]
     for k in range(1, seq):
         send(hidden, folded.at[mine_rows], 0, (lax.rem(mine_seq + k, seq), mine_tensor))
 
@@ -172,7 +193,6 @@
     own.start()
 
     wait(recv_sems, 0, folded.at[pl.ds(0, (seq - 1) * ROWS)])
-    half = width // 2
     for pair in range(seq // 2):
         both = folded[pair * 2 * ROWS : (pair + 1) * 2 * ROWS].astype(F32)
         rows = pl.ds(pair * ROWS, ROWS)
@@ -215,13 +235,17 @@
     target_logit = jnp.sum(stats[:, 2, :], axis=0, keepdims=True)
     log_prob = target_logit - row_top - jnp.log(row_total)
     sign = jnp.where(branch[...] == 1, 1.0, 0.0) - jnp.where(branch[...] == 2, 1.0, 0.0)
-    pairs = pair_weight.shape[0]
+    pairs = pair_weight_row.shape[1]
+    same = lax.broadcasted_iota(jnp.int32, (pairs, pairs), 0) == lax.broadcasted_iota(
+        jnp.int32, (pairs, pairs), 1
+    )
+    pair_weight = jnp.sum(jnp.where(same, pair_weight_row[...], 0.0), axis=1, keepdims=True)
     member = lax.broadcasted_iota(jnp.int32, (pairs, resp), 0) == pair_of_row[...]
     margin = jnp.sum(jnp.where(member, sign * (log_prob - ref_log_prob[...]), 0.0), axis=1, keepdims=True)
     z = -dpo_beta * margin
     softplus = jnp.maximum(z, 0.0) + jnp.log1p(jnp.exp(-jnp.abs(z)))
-    loss[...] = jnp.sum(pair_weight[...] * softplus, axis=0, keepdims=True)
-    push_back = pair_weight[...] * lax.logistic(z)
+    loss[...] = jnp.sum(pair_weight * softplus, axis=0, keepdims=True)
+    push_back = pair_weight * lax.logistic(z)
     row_scale = -dpo_beta * sign * jnp.sum(jnp.where(member, push_back, 0.0), axis=0, keepdims=True)
     probs = jnp.exp(value - row_top) / row_total
     rounded = (row_scale * (jnp.where(hit, 1.0, 0.0) - probs)).astype(BF16)
@@ -282,13 +306,9 @@
     came = came == lax.broadcasted_iota(jnp.int32, (n, slots), 0)
     sent_labels = stats[:, 3, :]
     tags[...] = jnp.zeros_like(tags)
-    for k in range(parts + 1):
-        if k == 0:
-            chosen = (column == wanted) & (column < capacity)
-        else:
-            chosen = (column >= capacity) & (wanted == (column - capacity) * parts + (k - 1))
-        spread = exact_dot(sent_labels, jnp.where(chosen, 1.0, 0.0), (((1,), (0,)), ((), ())))
-        tags[k : k + 1, :] = jnp.sum(jnp.where(came, spread, 0.0), axis=0, keepdims=True)
+    chosen = (column == wanted) & (column < capacity)
+    spread = exact_dot(sent_labels, jnp.where(chosen, 1.0, 0.0), (((1,), (0,)), ((), ())))
+    tags[0:1, :] = jnp.sum(jnp.where(came, spread, 0.0), axis=0, keepdims=True)
 
     own.wait()
 
@@ -307,18 +327,20 @@
         vocab = lax.broadcasted_iota(jnp.int32, (vocab_rows, count), 0).astype(F32) + 1.0
         main_pick = jnp.where(vocab == tags[0:1, :count], 1.0, 0.0).astype(BF16)
         subs = piece_width // block
-        rest[...] = jnp.zeros_like(rest)
+        picks = [unpack_pick(capacity, parts, part) for part in range(parts)]
+        for sub in range(subs):
+            for low in range(0, count, CHUNK):
+                last = jnp.zeros((CHUNK, block), F32)
+                for part in range(parts):
+                    here = pl.ds((part * subs + sub) * block, block)
+                    last = last + jnp.dot(picks[part], early[low : low + CHUNK, here], preferred_element_type=F32)
+                rest[sub, low : low + CHUNK, :] = last.astype(BF16)
         stores = []
         for i in range((parts + 1) * subs):
             here = pl.ds(i * block, block)
+            rows = early[:, here] if i < parts * subs else rest[i % subs]
             head = jnp.dot(dlogits[...], gathered[:, here], preferred_element_type=F32)
-            if i < parts * subs:
-                part = i // subs
-                last_pick = jnp.where(vocab == tags[part + 1 : part + 2, :count], 1.0, 0.0).astype(BF16)
-                base[i] = head + norm * jnp.dot(main_pick, early[:, here], preferred_element_type=F32)
-                rest[i % subs] += jnp.dot(last_pick, early[:, here], preferred_element_type=F32)
-            else:
-                base[i] = head + norm * rest[i % subs]
+            base[i] = head + norm * jnp.dot(main_pick, rows, preferred_element_type=F32)
             stores.append(pltpu.make_async_copy(base.at[i], base_hbm.at[i], base_sems.at[i]))
             stores[-1].start()
         for store in stores:
@@ -336,7 +358,7 @@
     wait(send_sems, 6, pieces.at[pl.ds(0, tensor - 1)])
 
 
-def weight_grad_kernel(parts, subs, skipped, norm, arrived, tags, dlogits, gathered, base, out, main_pick, rest):
+def weight_grad_kernel(capacity, parts, subs, skipped, norm, arrived, tags, dlogits, gathered, base, out, main_pick, rest):
     i = pl.program_id(0)
     vocab_rows, slots = main_pick.shape
     vocab = lax.broadcasted_iota(jnp.int32, (vocab_rows, slots), 0).astype(F32) + 1.0
@@ -352,17 +374,25 @@
         before = jnp.dot(dlogits[...], gathered[...], preferred_element_type=F32)
     sub = lax.rem(i, subs)
 
+    def store(rows):
+        out[...] = (before + norm * jnp.dot(main_pick[...], rows, preferred_element_type=F32)).astype(BF16)
+
     @pl.when(i < parts * subs)
     def _():
-        block = arrived[...]
-        out[...] = (before + norm * jnp.dot(main_pick[...], block, preferred_element_type=F32)).astype(BF16)
-        part = lax.div(i, subs)
-        last_pick = jnp.where(vocab == tags[pl.ds(part + 1, 1), :][:, skipped:], 1.0, 0.0).astype(BF16)
-        rest[pl.ds(sub, 1)] += jnp.dot(last_pick, block, preferred_element_type=F32)[None]
+        store(arrived[...])
+        pick = unpack_pick(capacity, parts, lax.div(i, subs))
+
+        def unpack(chunk, carry):
+            rows = pl.ds(pl.multiple_of(chunk * CHUNK, CHUNK), CHUNK)
+            moved = jnp.dot(pick, arrived[rows, :], preferred_element_type=F32)
+            rest[sub, rows, :] = (rest[sub, rows, :].astype(F32) + moved).astype(BF16)
+            return carry
+
+        lax.fori_loop(0, slots // CHUNK, unpack, 0)
 
     @pl.when(i >= parts * subs)
     def _():
-        out[...] = (before + norm * rest[pl.ds(sub, 1)][0]).astype(BF16)
+        store(rest[sub])
 
 
 def shards(
@@ -380,7 +410,6 @@
     packed_width = parts * piece * LANES
     slab = (tiles + tensor - 1) // tensor * LANES
     half = width // 2
-    folded = jnp.concatenate([hidden[:, :half], hidden[:, half:]], axis=0)
     vmem, hbm = pl.BlockSpec(memory_space=pltpu.VMEM), pl.BlockSpec(memory_space=pl.ANY)
     norm = math.sqrt(width)
     slots = n * ROWS
@@ -391,7 +420,7 @@
     early_scratch = [
         pltpu.VMEM((skipped, packed_width), BF16),
         pltpu.VMEM(base_shape, F32),
-        pltpu.VMEM((subs, vocab_rows, block), F32),
+        pltpu.VMEM((subs, skipped, block), BF16),
         pltpu.SemaphoreType.DMA((steps,)),
     ]
     arrived, base, tags, dlogits, gathered, hidden_grad, loss = pl.pallas_call(
@@ -405,11 +434,12 @@
             jax.ShapeDtypeStruct(hidden.shape, BF16),
             jax.ShapeDtypeStruct((1, 1), F32),
         ),
-        in_specs=[vmem] * 9 + [hbm],
+        in_specs=[vmem] * 8 + [hbm],
         out_specs=(hbm, hbm, vmem, vmem, vmem, vmem, vmem),
         scratch_shapes=[
             pltpu.VMEM((vocab_rows, width), BF16),
             pltpu.VMEM((slots, packed_width), BF16),
+            pltpu.VMEM((ROWS, half), BF16),
             pltpu.VMEM((seq * ROWS, half), BF16),
             pltpu.VMEM((vocab_rows, resp), F32),
             pltpu.VMEM((n, 8, resp), F32),
@@ -435,16 +465,15 @@
         branch.reshape(1, resp),
         pair_of_row.reshape(1, resp),
         ref_log_prob.reshape(1, resp),
-        pair_weight.reshape(pairs, 1),
+        pair_weight.reshape(1, pairs),
         token_ids.reshape(1, tokens),
-        token_ids.reshape(tokens, 1),
-        folded,
+        hidden,
         token_grad,
         weight,
     )
     last = parts * subs - 1
     weight_grad = pl.pallas_call(
-        functools.partial(weight_grad_kernel, parts, subs, skipped, norm),
+        functools.partial(weight_grad_kernel, capacity, parts, subs, skipped, norm),
         grid=(steps,),
         out_shape=jax.ShapeDtypeStruct(weight.shape, BF16),
         in_specs=[
@@ -457,7 +486,7 @@
         out_specs=pl.BlockSpec((vocab_rows, block), lambda i: (0, i)),
         scratch_shapes=[
             pltpu.VMEM((vocab_rows, slots - skipped), BF16),
-            pltpu.VMEM((subs, vocab_rows, block), F32),
+            pltpu.VMEM((subs, slots - skipped, block), BF16),
         ],
         compiler_params=pltpu.CompilerParams(vmem_limit_bytes=56 << 20),
         name="weight_grad",

time: 146 us -> 141 us (0.966)
  local copies, waits for them, and re-layouts: 4.22 us -> 0.64 us
    reshape x2 -> x0, local copies, waits for them, and re-layouts: 2.77 us -> none  [the longest x1 1.44 us: shards(): token_ids.reshape(tokens, 1)]
where the time goes in v5:
time: 141 us; the launch traced here: 140 us
  Pallas kernels  137 us (97%)
  between operations  2.36 us (2%)
    pallas_call x1, Pallas kernels, shards(): pl.pallas_call(functools.partial(exchange_kernel, seq, tensor, capacity,...  127 us
    pallas_call x1, Pallas kernels, shards(): pl.pallas_call(functools.partial(weight_grad_kernel, capacity, parts, sub...  9.69 us

profile of v5, /device:TPU:0, one launch (start us, length us, event | category | flops | bytes accessed | tf_op | source)
XLA Modules:
  0.0 139.9 jit_solution(11275601128789599869)
XLA Ops:
  0.6 127.2 %exchange.1 = (bf16[128,4480]{1,0:T(8,128)(2,1)}, f32[6,512,896]{2,1,0:T(8,128)}, f32[8,512]{1,0:T(8,128)}, bf16[512,64]{1,0:T(8,128)(2,1)}, bf16[64,5376]{1,0:T...) custom-call(s32[1,64]{1,0:T(1,128)} %bitcast.8, s32[1,64]{1,0:T(1,128)} %bitcast.9, s32[1,64]{1,0:T(1,128)} %bitcast.10, ...), custom_call_target="tpu_custom_call" | custom-call | tf_op jit(solution)/shard_map/exchange/pallas_call | solution.py:426
  127.9 0.0 copy-start
  127.9 9.7 %weight_grad.1 = bf16[512,5376]{1,0:T(8,128)(2,1)} custom-call(bf16[128,4480]{1,0:T(8,128)(2,1)} %get-tuple-element.11.arrived, f32[8,512]{1,0:T(8,128)} %get-tuple-element.12.tags, bf16[512,64]{1,0:T(8,128)(2,1)} %get-tuple-element.13.dlogits, bf16[64,5376]{1,0:T(8,128)(2,1)} %get-tuple-element.14.gathered, f32[6,512,896]{2,1,0:T(8,128)} %get-tuple-element.15.base), custom_call_target="tpu_custom_call" | custom-call | tf_op jit(solution)/shard_map/weight_grad/pallas_call | solution.py:475
  138.1 0.0 copy-done
  138.1 0.6 copy.15
Async XLA Ops:
  127.9 10.3 %copy-start = (bf16[8,5376]{1,0:T(8,128)(2,1)S(1)}, bf16[8,5376]{1,0:T(8,128)(2,1)}, u32[]{:S(2)}) copy-start(bf16[8,5376]{1,0:T(8,128)(2,1)} %get-tuple-element.22) | copy-start | bytes 258052

commit v6 on v5

--- a/solution.py
+++ b/solution.py
@@ -187,7 +187,8 @@
             lax.fori_loop(eighth * n // 8, (eighth + 1) * n // 8, send_block, 0)
 
     pack_wave(0)
-    send_blocks(0, 1)
+    send_blocks(0, 2)
+    pack_wave(1)
     own_rows = pl.ds(pl.multiple_of(own_block * ROWS, ROWS), ROWS)
     own = pltpu.make_async_copy(packed.at[own_rows], (early if early_waves else arrived).at[own_rows], own_sem)
     own.start()
@@ -226,8 +227,8 @@
         return carry
 
     lax.fori_loop(0, n, send_stat, 0)
-    send_blocks(1, 2)
-    pack_wave(1)
+    send_blocks(2, 3)
+    pack_wave(2)
     wait(recv_sems, 3, stats.at[pl.ds(0, n - 1)])
     tops = stats[:, 0, :]
     row_top = jnp.max(tops, axis=0, keepdims=True)
@@ -263,8 +264,8 @@
         peer = lax.rem(mine_seq + k, seq)
         rows = pl.ds(pl.multiple_of(peer * share, share), share)
         send(partial.at[rows], seq_parts.at[mine_seq], 4, (peer, mine_tensor))
-    send_blocks(2, 4)
-    pack_wave(2)
+    send_blocks(3, 5)
+    pack_wave(3)
     rows = pl.ds(pl.multiple_of(mine_seq * share, share), share)
     seq_parts[pl.ds(mine_seq, 1)] = partial[rows, :][None]
     wait(recv_sems, 4, seq_parts.at[pl.ds(0, seq - 1)])
@@ -279,8 +280,7 @@
     for k in range(1, tensor):
         peer = lax.rem(mine_tensor + k, tensor)
         send(sums.at[peer], tensor_parts.at[mine_tensor], 5, (mine_seq, peer))
-    send_blocks(4, 5)
-    pack_wave(3)
+    send_blocks(5, 6)
     tensor_parts[pl.ds(mine_tensor, 1)] = sums[pl.ds(mine_tensor, 1)]
     wait(recv_sems, 5, tensor_parts.at[pl.ds(0, tensor - 1)])
     total = tensor_parts[0]
@@ -290,7 +290,7 @@
     pieces[pl.ds(mine_tensor, 1)] = total[None]
     for k in range(1, tensor):
         send(done, pieces.at[mine_tensor], 6, (mine_seq, lax.rem(mine_tensor + k, tensor)))
-    send_blocks(5, 8)
+    send_blocks(6, 8)
 
     slots = n * ROWS
     column = lax.broadcasted_iota(jnp.int32, (resp, slots), 1)

time: 141 us -> 137 us (0.972)
  Pallas kernels: 137 us -> 133 us
    pallas_call x1, Pallas kernels: 127 us -> 123 us  [shards(): pl.pallas_call(functools.partial(exchange_kernel, seq, tensor, capacity,...]
where the time goes in v6:
time: 137 us; the launch traced here: 136 us
  Pallas kernels  133 us (97%)
  between operations  2.36 us (2%)
    pallas_call x1, Pallas kernels, shards(): pl.pallas_call(functools.partial(exchange_kernel, seq, tensor, capacity,...  123 us
    pallas_call x1, Pallas kernels, shards(): pl.pallas_call(functools.partial(weight_grad_kernel, capacity, parts, sub...  9.69 us

profile of v6, /device:TPU:0, one launch (start us, length us, event | category | flops | bytes accessed | tf_op | source)
XLA Modules:
  0.0 136.0 jit_solution(11151992077579501599)
XLA Ops:
  0.6 123.3 %exchange.1 = (bf16[128,4480]{1,0:T(8,128)(2,1)}, f32[6,512,896]{2,1,0:T(8,128)}, f32[8,512]{1,0:T(8,128)}, bf16[512,64]{1,0:T(8,128)(2,1)}, bf16[64,5376]{1,0:T...) custom-call(s32[1,64]{1,0:T(1,128)} %bitcast.8, s32[1,64]{1,0:T(1,128)} %bitcast.9, s32[1,64]{1,0:T(1,128)} %bitcast.10, ...), custom_call_target="tpu_custom_call" | custom-call | tf_op jit(solution)/shard_map/exchange/pallas_call | solution.py:426
  124.0 0.0 copy-start
  124.0 9.7 %weight_grad.1 = bf16[512,5376]{1,0:T(8,128)(2,1)} custom-call(bf16[128,4480]{1,0:T(8,128)(2,1)} %get-tuple-element.11.arrived, f32[8,512]{1,0:T(8,128)} %get-tuple-element.12.tags, bf16[512,64]{1,0:T(8,128)(2,1)} %get-tuple-element.13.dlogits, bf16[64,5376]{1,0:T(8,128)(2,1)} %get-tuple-element.14.gathered, f32[6,512,896]{2,1,0:T(8,128)} %get-tuple-element.15.base), custom_call_target="tpu_custom_call" | custom-call | tf_op jit(solution)/shard_map/weight_grad/pallas_call | solution.py:475
  134.2 0.0 copy-done
  134.2 0.6 copy.15
Async XLA Ops:
  124.0 10.3 %copy-start = (bf16[8,5376]{1,0:T(8,128)(2,1)S(1)}, bf16[8,5376]{1,0:T(8,128)(2,1)}, u32[]{:S(2)}) copy-start(bf16[8,5376]{1,0:T(8,128)(2,1)} %get-tuple-element.22) | copy-start | bytes 258052
